TPU v7x, 128 devices: a whole 4x4x4 slice. The times are simulated.
128 devices in a mesh: chain: 8 (over y, z_hi), resp: 16 (over x, z_lo, core).
Axes of the slice: x: 4, y: 4, z: 4 (z_hi: 2, z_lo: 2; z = z_hi * 2 + z_lo), core: 2. Of those that a mesh axis runs over, the one named last changes fastest.
Arguments:
- q_prompt: bfloat16 [4096, 8192], P('chain', 'resp'), may hold values from -8 to 8
- k_prompt: bfloat16 [4096, 1024], P(('chain', 'resp')), may hold values from -8 to 8
- v_prompt: bfloat16 [4096, 1024], P(('chain', 'resp')), may hold values from -6 to 6
- q_resp: bfloat16 [16, 512, 8192], P('resp', None, 'chain'), may hold values from -8 to 8
- k_resp: bfloat16 [16, 512, 1024], P('resp', None, 'chain'), may hold values from -6 to 6
- v_resp: bfloat16 [16, 512, 1024], P('resp', None, 'chain'), may hold values from -6 to 6
- tree_table: int32 [16, 8], P('resp'), may hold values from -1 to 6, as said below
- lengths: int32 [16], P('resp'), may hold values from 256 to 512, as said below
Outputs:
- prompt_out: bfloat16 [4096, 8192], P('chain', 'resp')
- resp_out: bfloat16 [16, 512, 8192], P('resp', None, 'chain')
Inputs may be any that keep to these rules, and one draw needn't show every extreme that they name: `tree_table`: entry j of a response's row is -1 (the block has no parent) or the index of an earlier block of that response; entry 0 is -1. `lengths`: some response has 512 live tokens.
All inputs are finite; a program needn't handle non-finite values.
Results may differ from a plain program's by a relative error of at most 0.009.
Values may be sent and summed in bfloat16 or wider, within the bound.
No kernel may reach another device: no remote copies, remote signals or barrier semaphores. Data moves between devices by JAX's collectives and lax.ppermute only.
A program may use at most 64 MiB of HBM per device.

v0:
```python
import functools

import jax
import jax.numpy as jnp
from jax import lax
from jax.experimental import pallas as pl
from jax.experimental.pallas import tpu as pltpu
from jax.sharding import PartitionSpec as P

QH = 64
KVH = 8
HD = 128
RBLK = 8
ROWS = 512
SUB = 32
GROUP = QH // KVH
STEP_HEADS = 4
SCALE = HD**-0.5 * 1.4426950408889634
LOW, HIGH = 1e-18, 1e30
AXES = ("chain", "resp")
STEPS = (0, 1, 3, 2)
CHUNKS = 4
MIB = 2**20
PLACES = [(y, z, x, k) for y in range(4) for z in range(4) for x in range(4) for k in range(2)]


def device_at(y, z, x, core):
    return (y * 2 + z // 2) * 16 + (x * 2 + z % 2) * 2 + core


def move(block, target):
    route = [(device_at(*p), device_at(*target(*p))) for p in PLACES]
    return lax.ppermute(block, AXES, route)


def first_axis(d):
    def target(y, z, x, core):
        return (y, z, (x + d) % 4, core) if core else ((y + d) % 4, z, x, core)

    return target


def along_z(d):
    return lambda y, z, x, core: (y, (z + d) % 4, x, core)


def last_axis(d):
    def target(y, z, x, core):
        return ((y + d) % 4, z, x, core) if core else (y, z, (x + d) % 4, core)

    return target


def other_core(y, z, x, core):
    return (y, z, x, 1 - core)


def dot_t(a, b):
    return lax.dot_general(a, b, (((1,), (1,)), ((), ())), preferred_element_type=jnp.float32)


def fold_rows(p):
    return jnp.sum(p.reshape(p.shape[0] // 8, 8, p.shape[1]), axis=0)


def online(carried, keys, values_t, queries, visible):
    run_max, run_sum, run_acc = carried
    scores = dot_t(keys, queries) * SCALE
    if visible is not None:
        scores = jnp.where(visible, scores, -1e30)
    new_max = jnp.maximum(run_max, jnp.max(scores, axis=0, keepdims=True))
    weights = jnp.exp2(scores - new_max)
    if visible is not None:
        weights = jnp.where(visible, weights, 0.0)
    rescale = jnp.exp2(run_max - new_max)
    run_sum = run_sum * rescale + jnp.sum(weights, axis=0, keepdims=True)
    added = jnp.dot(values_t, weights.astype(jnp.bfloat16), preferred_element_type=jnp.float32)
    return (new_max, run_sum, run_acc * rescale + added)


def fresh(cols):
    return (
        jnp.full((1, cols), -1e30, jnp.float32),
        jnp.zeros((1, cols), jnp.float32),
        jnp.zeros((HD, cols), jnp.float32),
    )


def tree_seen(tree_ref, len_ref):
    lines = []
    for j in range(RBLK):
        parent = tree_ref[0, j]
        line = jnp.int32(1 << j)
        for i in range(j):
            line = line | jnp.where(parent == i, lines[i], 0)
        lines.append(line)
    key_at = lax.broadcasted_iota(jnp.int32, (ROWS, ROWS), 0)
    row_at = lax.broadcasted_iota(jnp.int32, (ROWS, ROWS), 1)
    span = ROWS // RBLK
    line_of_row = jnp.zeros((ROWS, ROWS), jnp.int32)
    for j in range(RBLK):
        line_of_row = jnp.where(row_at // span == j, lines[j], line_of_row)
    related = (lax.shift_right_logical(line_of_row, key_at // span) & 1) == 1
    return related & (key_at <= row_at) & (key_at < len_ref[0])


def weigh(keys, queries, values_t, shown=None):
    scores = dot_t(keys, queries) * SCALE
    weights = jnp.exp2(scores if shown is None else scores + shown)
    added = jnp.dot(values_t, weights.astype(jnp.bfloat16), preferred_element_type=jnp.float32)
    return fold_rows(weights), added


def over_heads(one_head):
    def some(step, unused):
        for h in range(STEP_HEADS):
            head = step * STEP_HEADS + h
            one_head(head, pl.ds(pl.multiple_of(head * HD, HD), HD))
        return unused

    lax.fori_loop(0, GROUP // STEP_HEADS, some, 0)


def own_kernel(tree_ref, len_ref, q_ref, k_ref, v_ref, acc_ref, sum_ref, vt, seen):
    vt[...] = v_ref[...].T
    seen[...] = jnp.where(tree_seen(tree_ref, len_ref), 0.0, -jnp.inf)

    def one_head(h, cols):
        sum_ref[h], acc_ref[h] = weigh(k_ref[...], q_ref[:, cols], vt[...], seen[...])

    over_heads(one_head)


def pick_kernel(place_ref, own, k_other, v_other, *outs):
    near = jnp.where(place_ref[3] == 0, place_ref[0], place_ref[2])
    for step, out_ref in zip(STEPS, outs):
        width = 2 * HD
        cols = pl.ds(pl.multiple_of((near + step) % 4 * width, width), width)
        for i, other in enumerate((k_other, v_other)):
            out_ref[i, :SUB, :] = own[i, :, cols]
            out_ref[i, SUB:, :] = other[:, cols]


def arrange_kernel(*refs):
    out_ref = refs[4]
    for i, ref in enumerate(refs[:4]):
        for half in range(2):
            pieces = ref[2 * half : 2 * half + 2]
            out_ref[2 * i + half, 0] = pieces[:, 0].reshape(HD, HD)
            out_ref[2 * i + half, 1] = pieces[:, 1].reshape(HD, HD).T


def load_blocks(chunk, kb, vt):
    for b in range(8):
        kb[b * HD : (b + 1) * HD, :] = chunk[b, 0]
        vt[:, b * HD : (b + 1) * HD] = chunk[b, 1]


def load_chunk(from_here, here, other, kb, vt):
    @pl.when(from_here)
    def _():
        load_blocks(here, kb, vt)

    @pl.when(jnp.logical_not(from_here))
    def _():
        load_blocks(other, kb, vt)


def chunk_kernel(place_ref, q_ref, acc_in, sum_in, here, other, acc_ref, sum_ref, kb, vt):
    load_chunk(place_ref[3] == 0, here, other, kb, vt)

    def one_head(h, cols):
        sums, accs = weigh(kb[...], q_ref[:, cols], vt[...])
        sum_ref[h] = sum_in[h] + sums
        acc_ref[h] = acc_in[h] + accs

    over_heads(one_head)


def in_range(low, high):
    return (jnp.min(low) > LOW) & (jnp.max(high) < HIGH)


def prompt_part(place_ref, q_ref, acc_in, sum_in, held, out_ref, kb, vt, seen, acc, total, top):
    is_second = place_ref[3] == 1
    acc[...] = acc_in[...]
    total[...] = sum_in[...]

    def queries(h):
        return q_ref[:, h * HD : (h + 1) * HD]

    def earlier_pairs(body):
        def one_pair(i, unused):
            for at, spot in enumerate((1, 3, 2)):

                @pl.when(i == at)
                def _(spot=spot):
                    load_chunk(is_second, held[spot], held[CHUNKS + spot], kb, vt)

            body()
            return unused

        lax.fori_loop(0, place_ref[0], one_pair, 0)

    def add():
        for h in range(HALF_HEADS):
            sums, accs = weigh(kb[...], queries(h), vt[...])
            total[h] += sums
            acc[h] += accs

    earlier_pairs(add)

    def store(h, sums):
        shown = (acc[h] * (1.0 / sums)).astype(jnp.bfloat16)
        out_ref[:, h * HD : (h + 1) * HD] = shown.T

    low = high = jnp.ones((1, ROWS), jnp.float32)
    for h in range(HALF_HEADS):
        sums = jnp.sum(total[h], axis=0, keepdims=True)
        store(h, sums)
        low, high = jnp.minimum(low, sums), jnp.maximum(high, sums)

    @pl.when(jnp.logical_not(in_range(low, high)))
    def _():
        load_chunk(is_second, held[0], held[CHUNKS], kb, vt)
        for rows, visible in own_pair_seen(place_ref):
            seen[rows, :] = jnp.where(visible, 1.0, 0.0)
        top[...] = jnp.full_like(top, -1e30)
        total[...] = jnp.zeros_like(total)
        acc[...] = jnp.zeros_like(acc)

        def exact():
            def one_head(h, unused):
                cols = pl.ds(pl.multiple_of(h * HD, HD), HD)
                carried = (top[h], total[h, 0:1], acc[h])
                carried = online(carried, kb[...], vt[...], q_ref[:, cols], seen[...] > 0.5)
                top[h], total[h, 0:1], acc[h] = carried
                return unused

            lax.fori_loop(0, HALF_HEADS, one_head, 0)

        exact()
        seen[...] = jnp.ones_like(seen)
        earlier_pairs(exact)
        for h in range(HALF_HEADS):
            store(h, total[h, 0:1])


def last_kernel(place_ref, tree_ref, len_ref, q_ref, acc_in, sum_in, *refs):
    q_rows, acc_rows, sum_rows = refs[:3]
    rows_held, (k_own, v_own), refs = refs[3 : 3 + 2 * CHUNKS], refs[11:13], refs[13:]
    held, refs = refs[: 2 * CHUNKS], refs[2 * CHUNKS :]
    out_ref, out_rows, kb, vt, low, high, block, own = refs[:8]
    prompt_part(place_ref, q_rows, acc_rows, sum_rows, rows_held, out_rows, *refs[8:])
    here, other = rows_held[CHUNKS - 1], rows_held[2 * CHUNKS - 1]
    is_first = place_ref[3] == 0
    load_chunk(is_first, here, other, kb, vt)
    low[...] = jnp.full_like(low, 1.0)
    high[...] = jnp.full_like(high, 1.0)
    live = lax.broadcasted_iota(jnp.int32, (HD, ROWS), 1) < len_ref[0]

    def store(cols, acc, total):
        shown = jnp.where(live, acc * (1.0 / total), 0.0)
        out_ref[:, cols] = shown.astype(jnp.bfloat16).T

    def one_head(h, cols):
        sums, accs = weigh(kb[...], q_ref[:, cols], vt[...])
        total = jnp.sum(sum_in[h] + sums, axis=0, keepdims=True)
        low[...] = jnp.minimum(low[...], total)
        high[...] = jnp.maximum(high[...], total)
        store(cols, acc_in[h] + accs, total)

    over_heads(one_head)

    @pl.when(jnp.logical_not(in_range(low[...], high[...])))
    def _():
        pltpu.sync_copy(k_own, own.at[0])
        pltpu.sync_copy(v_own, own.at[1])

        def exact_head(h, unused):
            cols = pl.ds(pl.multiple_of(h * HD, HD), HD)
            queries = q_ref[:, cols]

            def one_block(i, carried, one, two):
                @pl.when(is_first)
                def _():
                    pltpu.sync_copy(one.at[i], block)

                @pl.when(jnp.logical_not(is_first))
                def _():
                    pltpu.sync_copy(two.at[i], block)

                return online(carried, block[0], block[1], queries, None)

            carried = fresh(ROWS)
            for one, two in zip(held[:CHUNKS], held[CHUNKS:]):
                carried = lax.fori_loop(
                    0, 8, functools.partial(one_block, one=one, two=two), carried
                )
            visible = tree_seen(tree_ref, len_ref)
            run_max, run_sum, run_acc = online(carried, own[0], own[1].T, queries, visible)
            store(cols, run_acc, run_sum)
            return unused

        lax.fori_loop(0, GROUP, exact_head, 0)


def own_pair_seen(place_ref):
    y, z, x, core = (place_ref[i] for i in range(4))
    row_at = lax.broadcasted_iota(jnp.int32, (SUB, ROWS), 1) + z // 2 * ROWS
    key_at = lax.broadcasted_iota(jnp.int32, (SUB, ROWS), 0)
    for i, z_step in enumerate(STEPS):
        for j, x_step in enumerate(STEPS):
            x0, z0 = (x - x_step) % 4, (z - z_step) % 4
            for lane in range(2):
                first = (z0 // 2) * ROWS + ((x0 * 2 + z0 % 2) * 2 + 1 - lane) * SUB
                at = ((i * 4 + j) * 2 + lane) * SUB
                yield slice(at, at + SUB), key_at + first <= row_at


def here_kernel(place_ref, q_ref, q_rows, acc_in, sum_in, here, other, *refs):
    acc_ref, sum_ref, acc_rows, sum_rows, kb, vt, kb_rows, vt_rows, seen = refs
    chunk_kernel(place_ref, q_ref, acc_in, sum_in, here, other, acc_ref, sum_ref, kb, vt)
    load_chunk(place_ref[3] == 1, here, other, kb_rows, vt_rows)
    for rows, visible in own_pair_seen(place_ref):
        seen[rows, :] = jnp.where(visible, 0.0, -jnp.inf)
    for h in range(HALF_HEADS):
        queries = q_rows[:, h * HD : (h + 1) * HD]
        sum_rows[h], acc_rows[h] = weigh(kb_rows[...], queries, vt_rows[...], seen[...])


HALF_HEADS = GROUP // 2
PAIR = 2 * ROWS
CHUNK = jax.ShapeDtypeStruct((8, 2, HD, HD), jnp.bfloat16)


def state_of(heads):
    return (
        jax.ShapeDtypeStruct((heads, HD, ROWS), jnp.float32),
        jax.ShapeDtypeStruct((heads, 8, ROWS), jnp.float32),
    )


SCALAR = pl.BlockSpec(memory_space=pltpu.SMEM)
VMEM = pl.BlockSpec(memory_space=pltpu.VMEM)
ANYWHERE = pl.BlockSpec(memory_space=pl.ANY)
KEYS = [pltpu.VMEM((PAIR, HD), jnp.bfloat16), pltpu.VMEM((HD, PAIR), jnp.bfloat16)]


def call(kernel, name, in_specs, out_shape, scratch, rows, keys):
    single = not isinstance(out_shape, tuple)
    return pl.pallas_call(
        kernel,
        in_specs=in_specs,
        out_specs=VMEM if single else tuple(VMEM for _ in out_shape),
        out_shape=out_shape,
        scratch_shapes=scratch,
        cost_estimate=pl.CostEstimate(
            flops=8 * rows * keys * HD, bytes_accessed=6 * MIB, transcendentals=rows * keys
        ),
        compiler_params=pltpu.CompilerParams(vmem_limit_bytes=32 * MIB),
        name=name,
    )


def attend_own(tree, length, q, k, v):
    scratch = [pltpu.VMEM((HD, ROWS), jnp.bfloat16), pltpu.VMEM((ROWS, ROWS), jnp.float32)]
    specs = [SCALAR, SCALAR, VMEM, VMEM, VMEM]
    return call(own_kernel, "own_keys", specs, state_of(GROUP), scratch, GROUP * ROWS, ROWS)(
        tree, length, q, k, v
    )


def pick(place, own, k_other, v_other):
    out = tuple(jax.ShapeDtypeStruct((2, 2 * SUB, 2 * HD), jnp.bfloat16) for _ in STEPS)
    return call(pick_kernel, "pick", [SCALAR] + [VMEM] * 3, out, [], 8, 8)(
        place, own, k_other, v_other
    )


def arrange(parts):
    return call(arrange_kernel, "arrange", [VMEM] * 4, CHUNK, [], 8, 8)(*parts)


def attend_chunk(place, q, state, here, other, name):
    specs = [SCALAR] + [VMEM] * 5
    return call(chunk_kernel, name, specs, state_of(GROUP), KEYS, GROUP * ROWS, PAIR)(
        place, q, *state, here, other
    )


def attend_here(place, q, q_rows, state, here, other):
    scratch = KEYS + KEYS + [pltpu.VMEM((PAIR, ROWS), jnp.float32)]
    specs = [SCALAR] + [VMEM] * 6
    out = state_of(GROUP) + state_of(HALF_HEADS)
    outs = call(here_kernel, "here_keys", specs, out, scratch, 3 * HALF_HEADS * ROWS, PAIR)(
        place, q, q_rows, *state, here, other
    )
    return outs[:2], outs[2:]


def attend_last(place, tree, length, q, state, q_rows, state_rows, held, k_own, v_own):
    specs = [SCALAR] * 3 + [VMEM] * (6 + len(held)) + [ANYWHERE] * (2 + len(held))
    scratch = KEYS + [
        pltpu.VMEM((1, ROWS), jnp.float32),
        pltpu.VMEM((1, ROWS), jnp.float32),
        pltpu.VMEM((2, HD, HD), jnp.bfloat16),
        pltpu.VMEM((2, ROWS, HD), jnp.bfloat16),
    ]
    scratch += KEYS + [
        pltpu.VMEM((PAIR, ROWS), jnp.float32),
        pltpu.VMEM((HALF_HEADS, HD, ROWS), jnp.float32),
        pltpu.VMEM((HALF_HEADS, 8, ROWS), jnp.float32),
        pltpu.VMEM((HALF_HEADS, 1, ROWS), jnp.float32),
    ]
    out = (
        jax.ShapeDtypeStruct((ROWS, GROUP * HD), jnp.bfloat16),
        jax.ShapeDtypeStruct(q_rows.shape, jnp.bfloat16),
    )
    return call(last_kernel, "last_keys", specs, out, scratch, 2 * GROUP * ROWS, PAIR)(
        place, tree, length, q, *state, q_rows, *state_rows, *held, k_own, v_own, *held
    )


def after(value, *events):
    return lax.optimization_barrier((value, *events))[0]


def on_device(q_prompt, k_prompt, v_prompt, q_resp, k_resp, v_resp, tree_table, lengths):
    chain, resp = lax.axis_index("chain"), lax.axis_index("resp")
    y, z, x, core = chain // 2, chain % 2 * 2 + resp // 2 % 2, resp // 4, resp % 2
    place = jnp.stack([y, z, x, core]).astype(jnp.int32)
    q = q_resp[0]

    def cols(block, at, count):
        return lax.dynamic_slice_in_dim(block, at * count * HD, count * HD, block.ndim - 1)

    own = jnp.stack([k_prompt, v_prompt])
    over = pick(place, own, move(k_prompt, other_core), move(v_prompt, other_core))
    over = [over[0]] + [move(part, first_axis(d)) for part, d in zip(over[1:], STEPS[1:])]
    over = jnp.stack(over)

    def for_z(at):
        return cols(over, jnp.where(core == 0, at // 2, at % 2), 1)

    over_z = [for_z(z)] + [move(for_z((z + d) % 4), along_z(d)) for d in STEPS[1:]]
    state = attend_own(tree_table, lengths, after(q, over), k_resp[0], v_resp[0])
    here = arrange(after(over_z, state[1]))
    here_o = move(here, other_core)
    left, right = move(here, last_axis(1)), move(here, last_axis(3))
    state, prompt_state = attend_here(place, q, q_prompt, state, here, here_o)
    left, right = after((left, right), state[1], prompt_state[1])
    left_o, right_o = move(left, other_core), move(right, other_core)
    far_l, far_r = move(left[:4], last_axis(1)), move(right[4:], last_axis(3))
    state = attend_chunk(place, q, state, left, left_o, "left_keys")
    far_l, far_r = after((far_l, far_r), state[1])
    far = jnp.concatenate([far_l, far_r])
    far_o = move(far, other_core)
    state = attend_chunk(place, q, state, right, right_o, "right_keys")
    held = (here, left, right, far, here_o, left_o, right_o, far_o)
    resp_out, prompt_out = attend_last(
        place, tree_table, lengths, q, state, q_prompt, prompt_state, held, k_resp[0], v_resp[0]
    )
    return (prompt_out, resp_out[None])


def solution(mesh):
    placed = (
        P("chain", "resp"),
        P(("chain", "resp"), None),
        P(("chain", "resp"), None),
        P("resp", None, "chain"),
        P("resp", None, "chain"),
        P("resp", None, "chain"),
        P("resp", None),
        P("resp"),
    )
    return jax.shard_map(
        on_device,
        mesh=mesh,
        in_specs=placed,
        out_specs=(P("chain", "resp"), P("resp", None, "chain")),
        check_vma=False,
    )
```

profile of v0, /device:TPU:25, one launch (start us, length us, event | category | flops | bytes accessed | tf_op | source)
XLA Modules:
  0.0 225.1 jit_solution(14309473514453507328)
XLA Ops:
  0.6 0.0 copy-start
  0.6 0.0 copy-start.4
  0.7 0.0 copy-start.2
  0.7 0.0 copy-start.3
  0.7 0.8 collective-permute-start
  1.4 0.1 collective-permute-start.1
  1.5 0.9 pad_maximum_fusion.1.own
  2.4 0.1 pad_add_fusion.place_ref
  2.5 0.1 collective-permute-done.k_other
  2.5 0.4 collective-permute-done.1.v_other
  2.9 0.6 pick.1
  3.5 2.8 %collective-permute-start.4 = (bf16[2,64,256]{2,1,0:T(8,128)(2,1)S(1)}, bf16[2,64,256]{2,1,0:T(8,128)(2,1)S(1)}, u32[]{:S(2)}, u32[]{:S(2)}) collective-permute-start(bf16[2,64,256]{2,1,0:T(8,128)(2,1)S(1)} %get-tuple-element.30), channel_id=1, source_target_pairs={{0,64},{1,9},{4,68},{5,13},{8,72},{9,1},{12,76},{13,5},{2,66},{3,1... | collective-permute-start | bytes 196616 | tf_op jit(solution)/shard_map/ppermute | solution.py:33
  6.3 0.9 collective-permute-start.3
  7.2 0.6 collective-permute-start.2
  8.4 0.0 collective-permute-done.4
  8.5 1.2 collective-permute-done.3
  9.7 1.8 collective-permute-done.2
  11.5 0.1 constant_dynamic-slice_fusion
  11.7 1.7 collective-permute-start.5
  13.4 2.2 collective-permute-start.6
  15.6 1.2 collective-permute-start.7
  16.8 0.0 copy-done
  16.8 0.0 copy-done.4
  16.8 0.0 copy-done.2
  16.8 0.0 copy-done.3
  16.8 0.0 copy-start.1
  16.8 4.0 %own_keys.1 = (f32[8,128,512]{2,1,0:T(8,128)S(1)}, f32[8,8,512]{2,1,0:T(8,128)S(1)}) custom-call(s32[1,8]{1,0:T(1,128)S(1)} %copy-done.4, s32[1]{0:T(128)S(6)} %copy.11.len_ref, bf16[512,1024]{1,0:T(8,128)(2,1)S(1)} %bitcast.15, bf16[512,128]{1,0:T(8,128)(2,1)S(1)} %bitcast.20, bf16[512,128]{1,0:T(8,128)(2,1)S(1)} %bitcast.22), custom_call_target="tpu_custom_call" | custom-call | flops 2147483648 | bytes 6291456 | tf_op jit(solution)/shard_map/own_keys/pallas_call | solution.py:369
  20.8 0.0 collective-permute-done.5.refs_1_
  20.8 0.3 collective-permute-done.6.refs_2_
  21.1 1.5 collective-permute-done.7.refs_3_
  22.6 0.1 arrange.1.here.refs_3_.refs_13_
  22.8 0.2 collective-permute-start.8
  23.0 1.5 collective-permute-start.9
  24.5 0.0 collective-permute-start.10
  24.5 0.2 collective-permute-done.8.other.refs_7_.refs_17_
  24.7 0.0 copy-done.1
  24.7 7.0 %here_keys.1 = (f32[8,128,512]{2,1,0:T(8,128)S(1)}, f32[8,8,512]{2,1,0:T(8,128)S(1)}, f32[4,128,512]{2,1,0:T(8,128)S(1)}, f32[4,8,512]{2,1,0:T(8,128)S(1)}) custom-call(s32[4]{0:T(128)S(1)} %pad_add_fusion.place_ref, bf16[512,1024]{1,0:T(8,128)(2,1)S(1)} %bitcast.16, bf16[512,512]{1,0:T(8,128)(2,1)S(1)} %copy-done.1, ...), custom_call_target="tpu_custom_call" | custom-call | flops 6442450944 | bytes 6291456 | tf_op jit(solution)/shard_map/here_keys/pallas_call | solution.py:396
  31.8 0.0 collective-permute-done.9.here.refs_4_.refs_14_
  31.8 2.0 collective-permute-done.10.here.refs_5_.refs_15_
  33.8 0.0 collective-permute-start.11
  33.8 0.6 collective-permute-start.12
  34.4 1.0 collective-permute-start.13
  35.4 0.6 collective-permute-start.14
  35.9 0.0 collective-permute-done.11.other.refs_8_.refs_18_
  35.9 4.8 %left_keys.1 = (f32[8,128,512]{2,1,0:T(8,128)S(1)}, f32[8,8,512]{2,1,0:T(8,128)S(1)}) custom-call(s32[4]{0:T(128)S(1)} %pad_add_fusion.place_ref, bf16[512,1024]{1,0:T(8,128)(2,1)S(1)} %bitcast.17, f32[8,128,512]{2,1,0:T(8,128)S(1)} %get-tuple-element.38.acc_in, f32[8,8,512]{2,1,0:T(8,128)S(1)} %get-tuple-element.39.sum_in, ...), custom_call_target="tpu_custom_call" | custom-call | flops 4294967296 | bytes 6291456 | tf_op jit(solution)/shard_map/left_keys/pallas_call | solution.py:387
  40.8 0.0 collective-permute-done.13
  40.8 1.0 collective-permute-done.14
  41.9 0.9 collective-permute-start.15
  42.8 0.0 collective-permute-done.12.other.refs_9_.refs_19_
  42.8 4.6 %right_keys.1 = (f32[8,128,512]{2,1,0:T(8,128)S(1)}, f32[8,8,512]{2,1,0:T(8,128)S(1)}) custom-call(s32[4]{0:T(128)S(1)} %pad_add_fusion.place_ref, bf16[512,1024]{1,0:T(8,128)(2,1)S(1)} %bitcast.18, f32[8,128,512]{2,1,0:T(8,128)S(1)} %get-tuple-element.42.acc_in, f32[8,8,512]{2,1,0:T(8,128)S(1)} %get-tuple-element.43.sum_in, ...), custom_call_target="tpu_custom_call" | custom-call | flops 4294967296 | bytes 6291456 | tf_op jit(solution)/shard_map/right_keys/pallas_call | solution.py:387
  47.4 0.0 collective-permute-done.15.refs_10_.refs_20_
  47.4 177.7 %last_keys.1 = (bf16[512,1024]{1,0:T(8,128)(2,1)}, bf16[512,512]{1,0:T(8,128)(2,1)}) custom-call(s32[4]{0:T(128)S(1)} %pad_add_fusion.place_ref, s32[1,8]{1,0:T(1,128)S(1)} %copy-done.4, s32[1]{0:T(128)S(6)} %copy.11.len_ref, bf16[512,1024]{1,0:T(8,128)(2,1)S(1)} %bitcast.19, f32[8,128,512]{2,1,0:T(8,128)S(1)} %get-tuple-element.45.acc_in, ...), custom_call_target="tpu_custom_call" | custom-call | flops 8589934592 | bytes 6291456 | tf_op jit(solution)/shard_map/last_keys/pallas_call | solution.py:420
  (5 shorter events, 0.1 us)
Async XLA Ops:
  0.6 16.2 %copy-start = (bf16[1,512,1024]{2,1,0:T(8,128)(2,1)S(1)}, bf16[1,512,1024]{2,1,0:T(8,128)(2,1)}, u32[]{:S(2)}) copy-start(bf16[1,512,1024]{2,1,0:T(8,128)(2,1)} %param.11) | copy-start | bytes 3145732
  0.6 16.1 %copy-start.4 = (s32[1,8]{1,0:T(1,128)S(1)}, s32[1,8]{1,0:T(1,128)}, u32[]{:S(2)}) copy-start(s32[1,8]{1,0:T(1,128)} %tree_ref.3) | copy-start | bytes 100
  0.7 16.1 %copy-start.2 = (bf16[1,512,128]{2,1,0:T(8,128)(2,1)S(1)}, bf16[1,512,128]{2,1,0:T(8,128)(2,1)}, u32[]{:S(2)}) copy-start(bf16[1,512,128]{2,1,0:T(8,128)(2,1)} %param.12) | copy-start | bytes 393220
  0.7 16.1 %copy-start.3 = (bf16[1,512,128]{2,1,0:T(8,128)(2,1)S(1)}, bf16[1,512,128]{2,1,0:T(8,128)(2,1)}, u32[]{:S(2)}) copy-start(bf16[1,512,128]{2,1,0:T(8,128)(2,1)} %param.13) | copy-start | bytes 393220
  0.7 1.9 collective-permute-start
  1.4 1.5 collective-permute-start.1
  3.5 5.0 %collective-permute-start.4 = (bf16[2,64,256]{2,1,0:T(8,128)(2,1)S(1)}, bf16[2,64,256]{2,1,0:T(8,128)(2,1)S(1)}, u32[]{:S(2)}, u32[]{:S(2)}) collective-permute-start(bf16[2,64,256]{2,1,0:T(8,128)(2,1)S(1)} %get-tuple-element.30), channel_id=1, source_target_pairs={{0,64},{1,9},{4,68},{5,13},{8,72},{9,1},{12,76},{13,5},{2,66},{3,1... | collective-permute-start | bytes 196616 | tf_op jit(solution)/shard_map/ppermute | solution.py:33
  6.3 3.4 %collective-permute-start.3 = (bf16[2,64,256]{2,1,0:T(8,128)(2,1)S(1)}, bf16[2,64,256]{2,1,0:T(8,128)(2,1)S(1)}, u32[]{:S(2)}, u32[]{:S(2)}) collective-permute-start(bf16[2,64,256]{2,1,0:T(8,128)(2,1)S(1)} %get-tuple-element.29), channel_id=1, source_target_pairs={{0,96},{1,13},{4,100},{5,1},{8,104},{9,5},{12,108},{13,9},{2,98},{... | collective-permute-start | bytes 196616 | tf_op jit(solution)/shard_map/ppermute | solution.py:33
  7.2 4.3 %collective-permute-start.2 = (bf16[2,64,256]{2,1,0:T(8,128)(2,1)S(1)}, bf16[2,64,256]{2,1,0:T(8,128)(2,1)S(1)}, u32[]{:S(2)}, u32[]{:S(2)}) collective-permute-start(bf16[2,64,256]{2,1,0:T(8,128)(2,1)S(1)} %get-tuple-element.28), channel_id=1, source_target_pairs={{0,32},{1,5},{4,36},{5,9},{8,40},{9,13},{12,44},{13,1},{2,34},{3,7... | collective-permute-start | bytes 196616 | tf_op jit(solution)/shard_map/ppermute | solution.py:33
  11.7 9.1 %collective-permute-start.5 = (bf16[4,2,64,128]{3,2,1,0:T(8,128)(2,1)S(1)}, bf16[4,2,64,128]{3,2,1,0:T(8,128)(2,1)S(1)}, u32[]{:S(2)}, u32[]{:S(2)}) collective-permute-start(bf16[4,2,64,128]{3,2,1,0:T(8,128)(2,1)S(1)} %get-tuple-element.54), channel_id=1, source_target_pairs={{0,2},{1,3},{4,6},{5,7},{8,10},{9,11},{12,14},{13,15},{2,16},{3,17... | collective-permute-start | bytes 393224 | tf_op jit(solution)/shard_map/ppermute | solution.py:33
  13.4 7.7 %collective-permute-start.6 = (bf16[4,2,64,128]{3,2,1,0:T(8,128)(2,1)S(1)}, bf16[4,2,64,128]{3,2,1,0:T(8,128)(2,1)S(1)}, u32[]{:S(2)}, u32[]{:S(2)}) collective-permute-start(bf16[4,2,64,128]{3,2,1,0:T(8,128)(2,1)S(1)} %get-tuple-element.53), channel_id=1, source_target_pairs={{0,18},{1,19},{4,22},{5,23},{8,26},{9,27},{12,30},{13,31},{2,0},{3... | collective-permute-start | bytes 393224 | tf_op jit(solution)/shard_map/ppermute | solution.py:33
  15.6 7.1 %collective-permute-start.7 = (bf16[4,2,64,128]{3,2,1,0:T(8,128)(2,1)S(1)}, bf16[4,2,64,128]{3,2,1,0:T(8,128)(2,1)S(1)}, u32[]{:S(2)}, u32[]{:S(2)}) collective-permute-start(bf16[4,2,64,128]{3,2,1,0:T(8,128)(2,1)S(1)} %get-tuple-element.52), channel_id=1, source_target_pairs={{0,16},{1,17},{4,20},{5,21},{8,24},{9,25},{12,28},{13,29},{2,18},{... | collective-permute-start | bytes 393224 | tf_op jit(solution)/shard_map/ppermute | solution.py:33
  16.8 7.9 %copy-start.1 = (bf16[512,512]{1,0:T(8,128)(2,1)S(1)}, bf16[512,512]{1,0:T(8,128)(2,1)}, u32[]{:S(2)}) copy-start(bf16[512,512]{1,0:T(8,128)(2,1)} %refs_0_.1) | copy-start | bytes 1572868
  22.8 2.0 collective-permute-start.8
  23.0 8.8 %collective-permute-start.9 = (bf16[8,2,128,128]{3,2,1,0:T(8,128)(2,1)S(1)}, bf16[8,2,128,128]{3,2,1,0:T(8,128)(2,1)S(1)}, u32[]{:S(2)}, u32[]{:S(2)}) collective-permute-start(bf16[8,2,128,128]{3,2,1,0:T(8,128)(2,1)S(1)} %arrange.1.here.refs_3_.refs_13_), channel_id=1, source_target_pairs={{0,4},{1,33},{4,8},{5,37},{8,12},{9,41},{12,0},{13,45},{2,6},{3,35... | collective-permute-start | bytes 1572872 | tf_op jit(solution)/shard_map/ppermute | solution.py:33
  24.5 9.2 %collective-permute-start.10 = (bf16[8,2,128,128]{3,2,1,0:T(8,128)(2,1)S(1)}, bf16[8,2,128,128]{3,2,1,0:T(8,128)(2,1)S(1)}, u32[]{:S(2)}, u32[]{:S(2)}) collective-permute-start(bf16[8,2,128,128]{3,2,1,0:T(8,128)(2,1)S(1)} %arrange.1.here.refs_3_.refs_13_), channel_id=1, source_target_pairs={{0,12},{1,97},{4,0},{5,101},{8,4},{9,105},{12,8},{13,109},{2,14},{... | collective-permute-start | bytes 1572872 | tf_op jit(solution)/shard_map/ppermute | solution.py:33
  33.8 2.2 collective-permute-start.11
  33.8 9.0 %collective-permute-start.12 = (bf16[8,2,128,128]{3,2,1,0:T(8,128)(2,1)S(1)}, bf16[8,2,128,128]{3,2,1,0:T(8,128)(2,1)S(1)}, u32[]{:S(2)}, u32[]{:S(2)}) collective-permute-start(bf16[8,2,128,128]{3,2,1,0:T(8,128)(2,1)S(1)} %collective-permute-done.10.here.refs_5_.refs_15_), channel_id=1, source_target_pairs={{0,1},{1,0},{4,5},{5,4},{8,9},{9,8},{12,13},{13,12},{2,3},{3,2},{6... | collective-permute-start | bytes 1572872 | tf_op jit(solution)/shard_map/ppermute | solution.py:33
  34.4 6.4 %collective-permute-start.13 = (bf16[4,2,128,128]{3,2,1,0:T(8,128)(2,1)S(1)}, bf16[4,2,128,128]{3,2,1,0:T(8,128)(2,1)S(1)}, u32[]{:S(2)}, u32[]{:S(2)}) collective-permute-start(bf16[4,2,128,128]{3,2,1,0:T(8,128)(2,1)S(1)} %slice.6), channel_id=1, source_target_pairs={{0,4},{1,33},{4,8},{5,37},{8,12},{9,41},{12,0},{13,45},{2,6},{3,35... | collective-permute-start | bytes 786440 | tf_op jit(solution)/shard_map/ppermute | solution.py:33
  35.4 6.4 %collective-permute-start.14 = (bf16[4,2,128,128]{3,2,1,0:T(8,128)(2,1)S(1)}, bf16[4,2,128,128]{3,2,1,0:T(8,128)(2,1)S(1)}, u32[]{:S(2)}, u32[]{:S(2)}) collective-permute-start(bf16[4,2,128,128]{3,2,1,0:T(8,128)(2,1)S(1)} %slice.7), channel_id=1, source_target_pairs={{0,12},{1,97},{4,0},{5,101},{8,4},{9,105},{12,8},{13,109},{2,14},{... | collective-permute-start | bytes 786440 | tf_op jit(solution)/shard_map/ppermute | solution.py:33
  41.9 5.5 %collective-permute-start.15 = (bf16[8,2,128,128]{3,2,1,0:T(8,128)(2,1)S(1)}, bf16[8,2,128,128]{3,2,1,0:T(8,128)(2,1)S(1)}, u32[]{:S(2)}, u32[]{:S(2)}) collective-permute-start(bf16[8,2,128,128]{3,2,1,0:T(8,128)(2,1)S(1)} %constant_dynamic-update-slice_fusion.refs_6_.refs_16_), channel_id=1, source_target_pairs={{0,1},{1,0},{4,5},{5,4},{8,9},{9,8},{12,13},{13,12},{2,3},{3,2},{6... | collective-permute-start | bytes 1572872 | tf_op jit(solution)/shard_map/ppermute | solution.py:33
where the time goes:
time: 225 us
  Pallas kernels  199 us (88%)
  starting transfers between devices  15 us (7%)
  waiting for transfers between devices  8.56 us (4%)
    pallas_call x1, Pallas kernels, attend_last(): call(last_kernel, 'last_keys', specs, out, scratch, 2 * GROUP * ROWS, PAIR)  178 us
    ppermute x16, starting transfers between devices, move(): return lax.ppermute(block, AXES, route)  15 us
    pallas_call x2, Pallas kernels, attend_chunk(): call(chunk_kernel, name, specs, state_of(GROUP), KEYS, GROUP * ROWS, PAIR)  9.45 us
    ppermute x16, waiting for transfers between devices, move(): return lax.ppermute(block, AXES, route)  8.56 us
    pallas_call x1, Pallas kernels, attend_here(): call(here_kernel, 'here_keys', specs, out, scratch, 3 * HALF_HEADS * ROWS...  7.01 us
  transfers between devices with their start and end apart: 16, of which 9 were waited for; matrix products, arithmetic and copies ran while one was open for 0% of the time, Pallas kernels for 9%

commit v1 on v0

--- a/solution.py
+++ b/solution.py
@@ -53,6 +53,11 @@
 
 def other_core(y, z, x, core):
     return (y, z, x, 1 - core)
+
+
+def coordinates():
+    chain, resp = lax.axis_index("chain"), lax.axis_index("resp")
+    return chain // 2, chain % 2 * 2 + resp // 2 % 2, resp // 4, resp % 2
 
 
 def dot_t(a, b):
@@ -121,8 +126,10 @@
     lax.fori_loop(0, GROUP // STEP_HEADS, some, 0)
 
 
-def own_kernel(tree_ref, len_ref, q_ref, k_ref, v_ref, acc_ref, sum_ref, vt, seen):
+def own_kernel(tree_ref, len_ref, q_ref, k_ref, v_ref, acc_ref, sum_ref, seen, live, vt):
     vt[...] = v_ref[...].T
+    rows = lax.broadcasted_iota(jnp.int32, live.shape, 1)
+    live[...] = jnp.where(rows < len_ref[0], 1.0, 0.0)
     seen[...] = jnp.where(tree_seen(tree_ref, len_ref), 0.0, -jnp.inf)
 
     def one_head(h, cols):
@@ -131,8 +138,9 @@
     over_heads(one_head)
 
 
-def pick_kernel(place_ref, own, k_other, v_other, *outs):
-    near = jnp.where(place_ref[3] == 0, place_ref[0], place_ref[2])
+def pick_kernel(own, k_other, v_other, *outs):
+    y, z, x, core = coordinates()
+    near = jnp.where(core == 0, y, x)
     for step, out_ref in zip(STEPS, outs):
         width = 2 * HD
         cols = pl.ds(pl.multiple_of((near + step) % 4 * width, width), width)
@@ -156,19 +164,29 @@
         vt[:, b * HD : (b + 1) * HD] = chunk[b, 1]
 
 
-def load_chunk(from_here, here, other, kb, vt):
-    @pl.when(from_here)
+def load_chunk(role, here, other, kb, vt):
+    core = coordinates()[3]
+
+    @pl.when(core == role)
     def _():
         load_blocks(here, kb, vt)
 
-    @pl.when(jnp.logical_not(from_here))
+    @pl.when(core != role)
     def _():
         load_blocks(other, kb, vt)
 
 
-def chunk_kernel(place_ref, q_ref, acc_in, sum_in, here, other, acc_ref, sum_ref, kb, vt):
-    load_chunk(place_ref[3] == 0, here, other, kb, vt)
-
+def load_sides(role, left, left_o, right, right_o, kb, vt):
+    load_chunk(role, left, left_o, kb.at[:PAIR], vt.at[:, :PAIR])
+    load_chunk(role, right, right_o, kb.at[PAIR:], vt.at[:, PAIR:])
+
+
+def wide_kernel(q_ref, acc_in, sum_in, left, left_o, right, right_o, acc_ref, sum_ref, kb, vt):
+    load_sides(0, left, left_o, right, right_o, kb, vt)
+    add_heads(q_ref, acc_in, sum_in, acc_ref, sum_ref, kb, vt)
+
+
+def add_heads(q_ref, acc_in, sum_in, acc_ref, sum_ref, kb, vt):
     def one_head(h, cols):
         sums, accs = weigh(kb[...], q_ref[:, cols], vt[...])
         sum_ref[h] = sum_in[h] + sums
@@ -181,34 +199,49 @@
     return (jnp.min(low) > LOW) & (jnp.max(high) < HIGH)
 
 
-def prompt_part(place_ref, q_ref, acc_in, sum_in, held, out_ref, kb, vt, seen, acc, total, top):
-    is_second = place_ref[3] == 1
-    acc[...] = acc_in[...]
-    total[...] = sum_in[...]
+def side_kernel(q_ref, acc_in, sum_in, left, left_o, right, right_o, acc_ref, sum_ref, kb, vt):
+    y = coordinates()[0]
+    load_sides(1, left, left_o, right, right_o, kb, vt)
+
+    def add(count):
+        for h in range(HALF_HEADS):
+            queries = q_ref[:, h * HD : (h + 1) * HD]
+            sums, accs = weigh(kb[:count], queries, vt[:, :count])
+            sum_ref[h] = sum_in[h] + sums
+            acc_ref[h] = acc_in[h] + accs
+
+    @pl.when(y == 3)
+    def _():
+        add(2 * PAIR)
+
+    @pl.when((y == 1) | (y == 2))
+    def _():
+        add(PAIR)
+
+    @pl.when(y == 0)
+    def _():
+        sum_ref[...] = sum_in[...]
+        acc_ref[...] = acc_in[...]
+
+
+def prompt_part(q_ref, acc_in, sum_in, held, out_ref, kb, vt, seen, acc, total, top):
+    y = coordinates()[0]
 
     def queries(h):
         return q_ref[:, h * HD : (h + 1) * HD]
 
-    def earlier_pairs(body):
-        def one_pair(i, unused):
-            for at, spot in enumerate((1, 3, 2)):
-
-                @pl.when(i == at)
-                def _(spot=spot):
-                    load_chunk(is_second, held[spot], held[CHUNKS + spot], kb, vt)
-
-            body()
-            return unused
-
-        lax.fori_loop(0, place_ref[0], one_pair, 0)
-
-    def add():
+    @pl.when(y >= 2)
+    def _():
+        load_chunk(1, held[3], held[CHUNKS + 3], kb, vt)
         for h in range(HALF_HEADS):
             sums, accs = weigh(kb[...], queries(h), vt[...])
-            total[h] += sums
-            acc[h] += accs
-
-    earlier_pairs(add)
+            total[h] = sum_in[h] + sums
+            acc[h] = acc_in[h] + accs
+
+    @pl.when(y < 2)
+    def _():
+        total[...] = sum_in[...]
+        acc[...] = acc_in[...]
 
     def store(h, sums):
         shown = (acc[h] * (1.0 / sums)).astype(jnp.bfloat16)
@@ -222,8 +255,8 @@
 
     @pl.when(jnp.logical_not(in_range(low, high)))
     def _():
-        load_chunk(is_second, held[0], held[CHUNKS], kb, vt)
-        for rows, visible in own_pair_seen(place_ref):
+        load_chunk(1, held[0], held[CHUNKS], kb, vt)
+        for rows, visible in own_pair_seen():
             seen[rows, :] = jnp.where(visible, 1.0, 0.0)
         top[...] = jnp.full_like(top, -1e30)
         total[...] = jnp.zeros_like(total)
@@ -241,23 +274,33 @@
 
         exact()
         seen[...] = jnp.ones_like(seen)
-        earlier_pairs(exact)
+
+        def one_pair(i, unused):
+            for at, spot in enumerate((1, 3, 2)):
+
+                @pl.when(i == at)
+                def _(spot=spot):
+                    load_chunk(1, held[spot], held[CHUNKS + spot], kb, vt)
+
+            exact()
+            return unused
+
+        lax.fori_loop(0, y, one_pair, 0)
         for h in range(HALF_HEADS):
             store(h, total[h, 0:1])
 
 
-def last_kernel(place_ref, tree_ref, len_ref, q_ref, acc_in, sum_in, *refs):
+def last_kernel(q_ref, acc_in, sum_in, live_ref, *refs):
     q_rows, acc_rows, sum_rows = refs[:3]
-    rows_held, (k_own, v_own), refs = refs[3 : 3 + 2 * CHUNKS], refs[11:13], refs[13:]
+    rows_held, (k_own, v_own, seen_own), refs = refs[3 : 3 + 2 * CHUNKS], refs[11:14], refs[14:]
     held, refs = refs[: 2 * CHUNKS], refs[2 * CHUNKS :]
     out_ref, out_rows, kb, vt, low, high, block, own = refs[:8]
-    prompt_part(place_ref, q_rows, acc_rows, sum_rows, rows_held, out_rows, *refs[8:])
-    here, other = rows_held[CHUNKS - 1], rows_held[2 * CHUNKS - 1]
-    is_first = place_ref[3] == 0
-    load_chunk(is_first, here, other, kb, vt)
+    prompt_part(q_rows, acc_rows, sum_rows, rows_held, out_rows, *refs[8:])
+    is_first = coordinates()[3] == 0
+    load_chunk(0, rows_held[CHUNKS - 1], rows_held[2 * CHUNKS - 1], kb, vt)
     low[...] = jnp.full_like(low, 1.0)
     high[...] = jnp.full_like(high, 1.0)
-    live = lax.broadcasted_iota(jnp.int32, (HD, ROWS), 1) < len_ref[0]
+    live = live_ref[0:1] > 0.5
 
     def store(cols, acc, total):
         shown = jnp.where(live, acc * (1.0 / total), 0.0)
@@ -276,6 +319,8 @@
     def _():
         pltpu.sync_copy(k_own, own.at[0])
         pltpu.sync_copy(v_own, own.at[1])
+        seen_buf = refs[10].at[:ROWS]
+        pltpu.sync_copy(seen_own, seen_buf)
 
         def exact_head(h, unused):
             cols = pl.ds(pl.multiple_of(h * HD, HD), HD)
@@ -297,7 +342,7 @@
                 carried = lax.fori_loop(
                     0, 8, functools.partial(one_block, one=one, two=two), carried
                 )
-            visible = tree_seen(tree_ref, len_ref)
+            visible = seen_buf[...] > -1.0
             run_max, run_sum, run_acc = online(carried, own[0], own[1].T, queries, visible)
             store(cols, run_acc, run_sum)
             return unused
@@ -305,8 +350,8 @@
         lax.fori_loop(0, GROUP, exact_head, 0)
 
 
-def own_pair_seen(place_ref):
-    y, z, x, core = (place_ref[i] for i in range(4))
+def own_pair_seen():
+    y, z, x, core = coordinates()
     row_at = lax.broadcasted_iota(jnp.int32, (SUB, ROWS), 1) + z // 2 * ROWS
     key_at = lax.broadcasted_iota(jnp.int32, (SUB, ROWS), 0)
     for i, z_step in enumerate(STEPS):
@@ -318,11 +363,12 @@
                 yield slice(at, at + SUB), key_at + first <= row_at
 
 
-def here_kernel(place_ref, q_ref, q_rows, acc_in, sum_in, here, other, *refs):
+def here_kernel(q_ref, q_rows, acc_in, sum_in, here, other, *refs):
     acc_ref, sum_ref, acc_rows, sum_rows, kb, vt, kb_rows, vt_rows, seen = refs
-    chunk_kernel(place_ref, q_ref, acc_in, sum_in, here, other, acc_ref, sum_ref, kb, vt)
-    load_chunk(place_ref[3] == 1, here, other, kb_rows, vt_rows)
-    for rows, visible in own_pair_seen(place_ref):
+    load_chunk(0, here, other, kb, vt)
+    add_heads(q_ref, acc_in, sum_in, acc_ref, sum_ref, kb, vt)
+    load_chunk(1, here, other, kb_rows, vt_rows)
+    for rows, visible in own_pair_seen():
         seen[rows, :] = jnp.where(visible, 0.0, -jnp.inf)
     for h in range(HALF_HEADS):
         queries = q_rows[:, h * HD : (h + 1) * HD]
@@ -344,7 +390,13 @@
 SCALAR = pl.BlockSpec(memory_space=pltpu.SMEM)
 VMEM = pl.BlockSpec(memory_space=pltpu.VMEM)
 ANYWHERE = pl.BlockSpec(memory_space=pl.ANY)
-KEYS = [pltpu.VMEM((PAIR, HD), jnp.bfloat16), pltpu.VMEM((HD, PAIR), jnp.bfloat16)]
+
+
+def keys_of(count):
+    return [pltpu.VMEM((count, HD), jnp.bfloat16), pltpu.VMEM((HD, count), jnp.bfloat16)]
+
+
+KEYS = keys_of(PAIR)
 
 
 def call(kernel, name, in_specs, out_shape, scratch, rows, keys):
@@ -364,43 +416,45 @@
 
 
 def attend_own(tree, length, q, k, v):
-    scratch = [pltpu.VMEM((HD, ROWS), jnp.bfloat16), pltpu.VMEM((ROWS, ROWS), jnp.float32)]
+    scratch = [pltpu.VMEM((HD, ROWS), jnp.bfloat16)]
     specs = [SCALAR, SCALAR, VMEM, VMEM, VMEM]
-    return call(own_kernel, "own_keys", specs, state_of(GROUP), scratch, GROUP * ROWS, ROWS)(
+    out = state_of(GROUP) + (
+        jax.ShapeDtypeStruct((ROWS, ROWS), jnp.float32),
+        jax.ShapeDtypeStruct((8, ROWS), jnp.float32),
+    )
+    outs = call(own_kernel, "own_keys", specs, out, scratch, GROUP * ROWS, ROWS)(
         tree, length, q, k, v
     )
-
-
-def pick(place, own, k_other, v_other):
+    return outs[:2], outs[2], outs[3]
+
+
+def pick(own, k_other, v_other):
     out = tuple(jax.ShapeDtypeStruct((2, 2 * SUB, 2 * HD), jnp.bfloat16) for _ in STEPS)
-    return call(pick_kernel, "pick", [SCALAR] + [VMEM] * 3, out, [], 8, 8)(
-        place, own, k_other, v_other
-    )
+    return call(pick_kernel, "pick", [VMEM] * 3, out, [], 8, 8)(own, k_other, v_other)
 
 
 def arrange(parts):
     return call(arrange_kernel, "arrange", [VMEM] * 4, CHUNK, [], 8, 8)(*parts)
 
 
-def attend_chunk(place, q, state, here, other, name):
-    specs = [SCALAR] + [VMEM] * 5
-    return call(chunk_kernel, name, specs, state_of(GROUP), KEYS, GROUP * ROWS, PAIR)(
-        place, q, *state, here, other
-    )
-
-
-def attend_here(place, q, q_rows, state, here, other):
+def attend_here(q, q_rows, state, here, other):
     scratch = KEYS + KEYS + [pltpu.VMEM((PAIR, ROWS), jnp.float32)]
-    specs = [SCALAR] + [VMEM] * 6
     out = state_of(GROUP) + state_of(HALF_HEADS)
-    outs = call(here_kernel, "here_keys", specs, out, scratch, 3 * HALF_HEADS * ROWS, PAIR)(
-        place, q, q_rows, *state, here, other
+    outs = call(here_kernel, "here_keys", [VMEM] * 6, out, scratch, 3 * HALF_HEADS * ROWS, PAIR)(
+        q, q_rows, *state, here, other
     )
     return outs[:2], outs[2:]
 
 
-def attend_last(place, tree, length, q, state, q_rows, state_rows, held, k_own, v_own):
-    specs = [SCALAR] * 3 + [VMEM] * (6 + len(held)) + [ANYWHERE] * (2 + len(held))
+def attend_sides(kernel, name, heads, q, state, sides):
+    scratch = keys_of(2 * PAIR)
+    return call(kernel, name, [VMEM] * 7, state_of(heads), scratch, heads * ROWS, 2 * PAIR)(
+        q, *state, *sides
+    )
+
+
+def attend_last(q, state, live, q_rows, state_rows, held, k_own, v_own, seen):
+    specs = [VMEM] * (7 + len(held)) + [ANYWHERE] * (3 + len(held))
     scratch = KEYS + [
         pltpu.VMEM((1, ROWS), jnp.float32),
         pltpu.VMEM((1, ROWS), jnp.float32),
@@ -418,7 +472,7 @@
         jax.ShapeDtypeStruct(q_rows.shape, jnp.bfloat16),
     )
     return call(last_kernel, "last_keys", specs, out, scratch, 2 * GROUP * ROWS, PAIR)(
-        place, tree, length, q, *state, q_rows, *state_rows, *held, k_own, v_own, *held
+        q, *state, live, q_rows, *state_rows, *held, k_own, v_own, seen, *held
     )
 
 
@@ -427,16 +481,14 @@
 
 
 def on_device(q_prompt, k_prompt, v_prompt, q_resp, k_resp, v_resp, tree_table, lengths):
-    chain, resp = lax.axis_index("chain"), lax.axis_index("resp")
-    y, z, x, core = chain // 2, chain % 2 * 2 + resp // 2 % 2, resp // 4, resp % 2
-    place = jnp.stack([y, z, x, core]).astype(jnp.int32)
+    y, z, x, core = coordinates()
     q = q_resp[0]
 
     def cols(block, at, count):
         return lax.dynamic_slice_in_dim(block, at * count * HD, count * HD, block.ndim - 1)
 
     own = jnp.stack([k_prompt, v_prompt])
-    over = pick(place, own, move(k_prompt, other_core), move(v_prompt, other_core))
+    over = pick(own, move(k_prompt, other_core), move(v_prompt, other_core))
     over = [over[0]] + [move(part, first_axis(d)) for part, d in zip(over[1:], STEPS[1:])]
     over = jnp.stack(over)
 
@@ -444,22 +496,25 @@
         return cols(over, jnp.where(core == 0, at // 2, at % 2), 1)
 
     over_z = [for_z(z)] + [move(for_z((z + d) % 4), along_z(d)) for d in STEPS[1:]]
-    state = attend_own(tree_table, lengths, after(q, over), k_resp[0], v_resp[0])
-    here = arrange(after(over_z, state[1]))
+    q = after(q, over)
+    state, seen, live = attend_own(tree_table, lengths, q, k_resp[0], v_resp[0])
+    over_z = after(over_z, live)
+    here = arrange(over_z)
     here_o = move(here, other_core)
     left, right = move(here, last_axis(1)), move(here, last_axis(3))
-    state, prompt_state = attend_here(place, q, q_prompt, state, here, here_o)
-    left, right = after((left, right), state[1], prompt_state[1])
+    state, rows_state = attend_here(q, q_prompt, state, here, here_o)
+    left, right = after((left, right), state[1])
     left_o, right_o = move(left, other_core), move(right, other_core)
     far_l, far_r = move(left[:4], last_axis(1)), move(right[4:], last_axis(3))
-    state = attend_chunk(place, q, state, left, left_o, "left_keys")
+    sides = (left, left_o, right, right_o)
+    state = attend_sides(wide_kernel, "wide_keys", GROUP, q, state, sides)
     far_l, far_r = after((far_l, far_r), state[1])
     far = jnp.concatenate([far_l, far_r])
     far_o = move(far, other_core)
-    state = attend_chunk(place, q, state, right, right_o, "right_keys")
-    held = (here, left, right, far, here_o, left_o, right_o, far_o)
+    rows_state = attend_sides(side_kernel, "side_rows", HALF_HEADS, q_prompt, rows_state, sides)
+    held = (here, left, right, far, here_o, left_o, right_o, after(far_o, rows_state[1]))
     resp_out, prompt_out = attend_last(
-        place, tree_table, lengths, q, state, q_prompt, prompt_state, held, k_resp[0], v_resp[0]
+        q, state, live, q_prompt, rows_state, held, k_resp[0], v_resp[0], seen
     )
     return (prompt_out, resp_out[None])
 

time: 225 us -> 225 us (level)
  starting transfers between devices: 15 us -> 20.1 us
  Pallas kernels: 199 us -> 196 us
  waiting for transfers between devices: 8.56 us -> 6.15 us
    ppermute x16, starting transfers between devices: 15 us -> 20.1 us  [move(): return lax.ppermute(block, AXES, route)]
    pallas_call x1, Pallas kernels: 178 us -> 174 us  [attend_last(): call(last_kernel, 'last_keys', specs, out, scratch, 2 * GROUP * ROWS, PAIR)]
    ppermute x16, waiting for transfers between devices: 8.56 us -> 6.15 us  [move(): return lax.ppermute(block, AXES, route)]
  transfers between devices with their start and end apart: 16 -> 16, of which waited for: 9 -> 6; matrix products, arithmetic and copies ran while one was open for 0% -> 0% of each run, Pallas kernels for 9% -> 10%
where the time goes in v1:
time: 225 us
  Pallas kernels  196 us (87%)
  starting transfers between devices  20.1 us (9%)
  waiting for transfers between devices  6.15 us (3%)
    pallas_call x1, Pallas kernels, attend_last(): call(last_kernel, 'last_keys', specs, out, scratch, 2 * GROUP * ROWS, PAIR)  174 us
    ppermute x16, starting transfers between devices, move(): return lax.ppermute(block, AXES, route)  20.1 us
    pallas_call x2, Pallas kernels, attend_sides(): call(kernel, name, [VMEM] * 7, state_of(heads), scratch, heads * ROWS, 2...  11 us
    pallas_call x1, Pallas kernels, attend_here(): call(here_kernel, 'here_keys', [VMEM] * 6, out, scratch, 3 * HALF_HEADS *...  6.47 us
    ppermute x16, waiting for transfers between devices, move(): return lax.ppermute(block, AXES, route)  6.15 us
  transfers between devices with their start and end apart: 16, of which 6 were waited for; matrix products, arithmetic and copies ran while one was open for 0% of the time, Pallas kernels for 10%

profile of v1, /device:TPU:25, one launch (start us, length us, event | category | flops | bytes accessed | tf_op | source)
XLA Modules:
  0.0 225.0 jit_solution(14550429233701528994)
XLA Ops:
  0.6 0.0 copy-start
  0.6 0.0 copy-start.2
  0.7 0.0 copy-start.3
  0.7 0.0 copy-start.4
  0.7 0.8 collective-permute-start
  1.4 0.1 collective-permute-start.1
  1.5 0.9 pad_maximum_fusion.1.own
  2.4 0.1 collective-permute-done.k_other
  2.5 0.4 collective-permute-done.1.v_other
  2.9 1.3 collective-permute-start.2
  4.2 1.5 collective-permute-start.3
  5.7 1.5 collective-permute-start.4
  7.9 0.0 collective-permute-done.2
  7.9 0.0 collective-permute-done.3
  7.9 2.7 %collective-permute-done.4 = bf16[2,64,256]{2,1,0:T(8,128)(2,1)S(1)} collective-permute-done((bf16[2,64,256]{2,1,0:T(8,128)(2,1)S(1)}, bf16[2,64,256]{2,1,0:T(8,128)(2,1)S(1)}, u32[]{:S(2)}, u32[]{:S(2)}) %collective-permute-start.4) | collective-permute-done | bytes 65568 | tf_op jit(solution)/shard_map/ppermute | solution.py:33
  10.6 0.1 constant_dynamic-slice_fusion
  10.7 1.7 collective-permute-start.5
  12.4 2.2 collective-permute-start.6
  14.6 1.2 collective-permute-start.7
  15.8 0.0 copy-done
  15.8 0.0 copy-done.2
  15.9 0.0 copy-done.3
  15.9 0.0 copy-done.4
  15.9 0.0 copy-start.1
  15.9 4.0 %own_keys.1 = (f32[8,128,512]{2,1,0:T(8,128)S(1)}, f32[8,8,512]{2,1,0:T(8,128)S(1)}, f32[512,512]{1,0:T(8,128)S(1)}, f32[8,512]{1,0:T(8,128)S(1)}) custom-call(s32[1,8]{1,0:T(1,128)S(1)} %copy-done.4, s32[1]{0:T(128)S(6)} %copy.11.len_ref, bf16[512,1024]{1,0:T(8,128)(2,1)S(1)} %bitcast.11, bf16[512,128]{1,0:T(8,128)(2,1)S(1)} %bitcast.15, ...), custom_call_target="tpu_custom_call" | custom-call | flops 2147483648 | bytes 6291456 | tf_op jit(solution)/shard_map/own_keys/pallas_call | solution.py:425
  19.8 0.0 collective-permute-done.5.refs_1_
  19.8 0.0 collective-permute-done.6.refs_2_
  19.8 1.9 collective-permute-done.7.refs_3_
  21.7 0.1 arrange.1.here.refs_3_.refs_14_
  21.9 1.3 collective-permute-start.8
  23.2 0.2 collective-permute-start.10
  23.4 2.5 %collective-permute-start.9 = (bf16[8,2,128,128]{3,2,1,0:T(8,128)(2,1)S(1)}, bf16[8,2,128,128]{3,2,1,0:T(8,128)(2,1)S(1)}, u32[]{:S(2)}, u32[]{:S(2)}) collective-permute-start(bf16[8,2,128,128]{3,2,1,0:T(8,128)(2,1)S(1)} %arrange.1.here.refs_3_.refs_14_), channel_id=1, source_target_pairs={{0,4},{1,33},{4,8},{5,37},{8,12},{9,41},{12,0},{13,45},{2,6},{3,35... | collective-permute-start | bytes 1572872 | tf_op jit(solution)/shard_map/ppermute | solution.py:33
  25.9 0.0 collective-permute-done.8.other.refs_7_.refs_18_
  25.9 0.0 copy-done.1
  25.9 6.5 %here_keys.1 = (f32[8,128,512]{2,1,0:T(8,128)S(1)}, f32[8,8,512]{2,1,0:T(8,128)S(1)}, f32[4,128,512]{2,1,0:T(8,128)S(1)}, f32[4,8,512]{2,1,0:T(8,128)S(1)}) custom-call(bf16[512,1024]{1,0:T(8,128)(2,1)S(1)} %bitcast.12, bf16[512,512]{1,0:T(8,128)(2,1)S(1)} %copy-done.1, f32[8,128,512]{2,1,0:T(8,128)S(1)} %get-tuple-element.35.acc_in, ...), custom_call_target="tpu_custom_call" | custom-call | flops 6442450944 | bytes 6291456 | tf_op jit(solution)/shard_map/here_keys/pallas_call | solution.py:443
  32.3 0.4 collective-permute-done.10.right.refs_5_.refs_16_
  32.7 0.0 collective-permute-done.9.left.refs_4_.refs_15_
  32.7 2.7 %collective-permute-start.11 = (bf16[8,2,128,128]{3,2,1,0:T(8,128)(2,1)S(1)}, bf16[8,2,128,128]{3,2,1,0:T(8,128)(2,1)S(1)}, u32[]{:S(2)}, u32[]{:S(2)}) collective-permute-start(bf16[8,2,128,128]{3,2,1,0:T(8,128)(2,1)S(1)} %collective-permute-done.9.left.refs_4_.refs_15_), channel_id=1, source_target_pairs={{0,1},{1,0},{4,5},{5,4},{8,9},{9,8},{12,13},{13,12},{2,3},{3,2},{6... | collective-permute-start | bytes 1572872 | tf_op jit(solution)/shard_map/ppermute | solution.py:33
  35.4 0.0 collective-permute-start.12
  35.5 1.0 collective-permute-start.13
  36.5 0.5 collective-permute-start.14
  37.0 0.0 collective-permute-done.11.left_o.refs_8_.refs_19_
  37.0 0.7 collective-permute-done.12.right_o.refs_9_.refs_20_
  37.7 7.3 %wide_keys.1 = (f32[8,128,512]{2,1,0:T(8,128)S(1)}, f32[8,8,512]{2,1,0:T(8,128)S(1)}) custom-call(bf16[512,1024]{1,0:T(8,128)(2,1)S(1)} %bitcast.13, f32[8,128,512]{2,1,0:T(8,128)S(1)} %get-tuple-element.42.acc_in, f32[8,8,512]{2,1,0:T(8,128)S(1)} %get-tuple-element.43.sum_in, bf16[8,2,128,128]{3,2,1,0:T(8,128)(2,1)S(1)} %collective-permute-done.9.left.refs_4_.refs_15_, ...), custom_call_target="tpu_custom_call" | custom-call | flops 8589934592 | bytes 6291456 | tf_op jit(solution)/shard_map/wide_keys/pallas_call | solution.py:451
  45.0 0.0 collective-permute-done.13
  45.1 0.0 collective-permute-done.14
  45.1 1.7 collective-permute-start.15
  46.8 3.6 %side_rows.1 = (f32[4,128,512]{2,1,0:T(8,128)S(1)}, f32[4,8,512]{2,1,0:T(8,128)S(1)}) custom-call(bf16[512,512]{1,0:T(8,128)(2,1)S(1)} %copy-done.1, f32[4,128,512]{2,1,0:T(8,128)S(1)} %get-tuple-element.48.acc_in, f32[4,8,512]{2,1,0:T(8,128)S(1)} %get-tuple-element.49.sum_in, bf16[8,2,128,128]{3,2,1,0:T(8,128)(2,1)S(1)} %collective-permute-done.9.left.refs_4_.refs_15_, ...), custom_call_target="tpu_custom_call" | custom-call | flops 4294967296 | bytes 6291456 | tf_op jit(solution)/shard_map/side_rows/pallas_call | solution.py:451
  50.5 0.0 collective-permute-done.15.refs_10_.refs_21_
  50.5 174.5 %last_keys.1 = (bf16[512,1024]{1,0:T(8,128)(2,1)}, bf16[512,512]{1,0:T(8,128)(2,1)}) custom-call(bf16[512,1024]{1,0:T(8,128)(2,1)S(1)} %bitcast.14, f32[8,128,512]{2,1,0:T(8,128)S(1)} %get-tuple-element.46.acc_in, f32[8,8,512]{2,1,0:T(8,128)S(1)} %get-tuple-element.47.sum_in, f32[8,512]{1,0:T(8,128)S(1)} %get-tuple-element.37.live_ref, ...), custom_call_target="tpu_custom_call" | custom-call | flops 8589934592 | bytes 6291456 | tf_op jit(solution)/shard_map/last_keys/pallas_call | solution.py:474
  (6 shorter events, 0.2 us)
Async XLA Ops:
  0.6 15.2 %copy-start = (bf16[1,512,1024]{2,1,0:T(8,128)(2,1)S(1)}, bf16[1,512,1024]{2,1,0:T(8,128)(2,1)}, u32[]{:S(2)}) copy-start(bf16[1,512,1024]{2,1,0:T(8,128)(2,1)} %param.11) | copy-start | bytes 3145732
  0.6 15.2 %copy-start.2 = (bf16[1,512,128]{2,1,0:T(8,128)(2,1)S(1)}, bf16[1,512,128]{2,1,0:T(8,128)(2,1)}, u32[]{:S(2)}) copy-start(bf16[1,512,128]{2,1,0:T(8,128)(2,1)} %param.12) | copy-start | bytes 393220
  0.7 15.2 %copy-start.3 = (bf16[1,512,128]{2,1,0:T(8,128)(2,1)S(1)}, bf16[1,512,128]{2,1,0:T(8,128)(2,1)}, u32[]{:S(2)}) copy-start(bf16[1,512,128]{2,1,0:T(8,128)(2,1)} %param.13) | copy-start | bytes 393220
  0.7 15.2 %copy-start.4 = (s32[1,8]{1,0:T(1,128)S(1)}, s32[1,8]{1,0:T(1,128)}, u32[]{:S(2)}) copy-start(s32[1,8]{1,0:T(1,128)} %tree_ref.1) | copy-start | bytes 100
  0.7 1.9 collective-permute-start
  1.4 1.5 collective-permute-start.1
  2.9 4.9 %collective-permute-start.2 = (bf16[2,64,256]{2,1,0:T(8,128)(2,1)S(1)}, bf16[2,64,256]{2,1,0:T(8,128)(2,1)S(1)}, u32[]{:S(2)}, u32[]{:S(2)}) collective-permute-start(bf16[2,64,256]{2,1,0:T(8,128)(2,1)S(1)} %get-tuple-element.31), channel_id=1, source_target_pairs={{0,32},{1,5},{4,36},{5,9},{8,40},{9,13},{12,44},{13,1},{2,34},{3,7... | collective-permute-start | bytes 196616 | tf_op jit(solution)/shard_map/ppermute | solution.py:33
  4.2 3.7 %collective-permute-start.3 = (bf16[2,64,256]{2,1,0:T(8,128)(2,1)S(1)}, bf16[2,64,256]{2,1,0:T(8,128)(2,1)S(1)}, u32[]{:S(2)}, u32[]{:S(2)}) collective-permute-start(bf16[2,64,256]{2,1,0:T(8,128)(2,1)S(1)} %get-tuple-element.32), channel_id=1, source_target_pairs={{0,96},{1,13},{4,100},{5,1},{8,104},{9,5},{12,108},{13,9},{2,98},{... | collective-permute-start | bytes 196616 | tf_op jit(solution)/shard_map/ppermute | solution.py:33
  5.7 4.9 %collective-permute-start.4 = (bf16[2,64,256]{2,1,0:T(8,128)(2,1)S(1)}, bf16[2,64,256]{2,1,0:T(8,128)(2,1)S(1)}, u32[]{:S(2)}, u32[]{:S(2)}) collective-permute-start(bf16[2,64,256]{2,1,0:T(8,128)(2,1)S(1)} %get-tuple-element.33), channel_id=1, source_target_pairs={{0,64},{1,9},{4,68},{5,13},{8,72},{9,1},{12,76},{13,5},{2,66},{3,1... | collective-permute-start | bytes 196616 | tf_op jit(solution)/shard_map/ppermute | solution.py:33
  10.7 9.1 %collective-permute-start.5 = (bf16[4,2,64,128]{3,2,1,0:T(8,128)(2,1)S(1)}, bf16[4,2,64,128]{3,2,1,0:T(8,128)(2,1)S(1)}, u32[]{:S(2)}, u32[]{:S(2)}) collective-permute-start(bf16[4,2,64,128]{3,2,1,0:T(8,128)(2,1)S(1)} %get-tuple-element.60), channel_id=1, source_target_pairs={{0,2},{1,3},{4,6},{5,7},{8,10},{9,11},{12,14},{13,15},{2,16},{3,17... | collective-permute-start | bytes 393224 | tf_op jit(solution)/shard_map/ppermute | solution.py:33
  12.4 7.4 %collective-permute-start.6 = (bf16[4,2,64,128]{3,2,1,0:T(8,128)(2,1)S(1)}, bf16[4,2,64,128]{3,2,1,0:T(8,128)(2,1)S(1)}, u32[]{:S(2)}, u32[]{:S(2)}) collective-permute-start(bf16[4,2,64,128]{3,2,1,0:T(8,128)(2,1)S(1)} %get-tuple-element.59), channel_id=1, source_target_pairs={{0,18},{1,19},{4,22},{5,23},{8,26},{9,27},{12,30},{13,31},{2,0},{3... | collective-permute-start | bytes 393224 | tf_op jit(solution)/shard_map/ppermute | solution.py:33
  14.6 7.1 %collective-permute-start.7 = (bf16[4,2,64,128]{3,2,1,0:T(8,128)(2,1)S(1)}, bf16[4,2,64,128]{3,2,1,0:T(8,128)(2,1)S(1)}, u32[]{:S(2)}, u32[]{:S(2)}) collective-permute-start(bf16[4,2,64,128]{3,2,1,0:T(8,128)(2,1)S(1)} %get-tuple-element.58), channel_id=1, source_target_pairs={{0,16},{1,17},{4,20},{5,21},{8,24},{9,25},{12,28},{13,29},{2,18},{... | collective-permute-start | bytes 393224 | tf_op jit(solution)/shard_map/ppermute | solution.py:33
  15.9 10.0 %copy-start.1 = (bf16[512,512]{1,0:T(8,128)(2,1)S(1)}, bf16[512,512]{1,0:T(8,128)(2,1)}, u32[]{:S(2)}) copy-start(bf16[512,512]{1,0:T(8,128)(2,1)} %refs_0_.1) | copy-start | bytes 1572868
  21.9 4.0 %collective-permute-start.8 = (bf16[8,2,128,128]{3,2,1,0:T(8,128)(2,1)S(1)}, bf16[8,2,128,128]{3,2,1,0:T(8,128)(2,1)S(1)}, u32[]{:S(2)}, u32[]{:S(2)}) collective-permute-start(bf16[8,2,128,128]{3,2,1,0:T(8,128)(2,1)S(1)} %arrange.1.here.refs_3_.refs_14_), channel_id=1, source_target_pairs={{0,1},{1,0},{4,5},{5,4},{8,9},{9,8},{12,13},{13,12},{2,3},{3,2},{6... | collective-permute-start | bytes 1572872 | tf_op jit(solution)/shard_map/ppermute | solution.py:33
  23.2 9.5 %collective-permute-start.10 = (bf16[8,2,128,128]{3,2,1,0:T(8,128)(2,1)S(1)}, bf16[8,2,128,128]{3,2,1,0:T(8,128)(2,1)S(1)}, u32[]{:S(2)}, u32[]{:S(2)}) collective-permute-start(bf16[8,2,128,128]{3,2,1,0:T(8,128)(2,1)S(1)} %arrange.1.here.refs_3_.refs_14_), channel_id=1, source_target_pairs={{0,12},{1,97},{4,0},{5,101},{8,4},{9,105},{12,8},{13,109},{2,14},{... | collective-permute-start | bytes 1572872 | tf_op jit(solution)/shard_map/ppermute | solution.py:33
  23.4 9.3 %collective-permute-start.9 = (bf16[8,2,128,128]{3,2,1,0:T(8,128)(2,1)S(1)}, bf16[8,2,128,128]{3,2,1,0:T(8,128)(2,1)S(1)}, u32[]{:S(2)}, u32[]{:S(2)}) collective-permute-start(bf16[8,2,128,128]{3,2,1,0:T(8,128)(2,1)S(1)} %arrange.1.here.refs_3_.refs_14_), channel_id=1, source_target_pairs={{0,4},{1,33},{4,8},{5,37},{8,12},{9,41},{12,0},{13,45},{2,6},{3,35... | collective-permute-start | bytes 1572872 | tf_op jit(solution)/shard_map/ppermute | solution.py:33
  32.7 4.3 %collective-permute-start.11 = (bf16[8,2,128,128]{3,2,1,0:T(8,128)(2,1)S(1)}, bf16[8,2,128,128]{3,2,1,0:T(8,128)(2,1)S(1)}, u32[]{:S(2)}, u32[]{:S(2)}) collective-permute-start(bf16[8,2,128,128]{3,2,1,0:T(8,128)(2,1)S(1)} %collective-permute-done.9.left.refs_4_.refs_15_), channel_id=1, source_target_pairs={{0,1},{1,0},{4,5},{5,4},{8,9},{9,8},{12,13},{13,12},{2,3},{3,2},{6... | collective-permute-start | bytes 1572872 | tf_op jit(solution)/shard_map/ppermute | solution.py:33
  35.4 2.3 %collective-permute-start.12 = (bf16[8,2,128,128]{3,2,1,0:T(8,128)(2,1)S(1)}, bf16[8,2,128,128]{3,2,1,0:T(8,128)(2,1)S(1)}, u32[]{:S(2)}, u32[]{:S(2)}) collective-permute-start(bf16[8,2,128,128]{3,2,1,0:T(8,128)(2,1)S(1)} %collective-permute-done.10.right.refs_5_.refs_16_), channel_id=1, source_target_pairs={{0,1},{1,0},{4,5},{5,4},{8,9},{9,8},{12,13},{13,12},{2,3},{3,2},{6... | collective-permute-start | bytes 1572872 | tf_op jit(solution)/shard_map/ppermute | solution.py:33
  35.5 9.6 %collective-permute-start.13 = (bf16[4,2,128,128]{3,2,1,0:T(8,128)(2,1)S(1)}, bf16[4,2,128,128]{3,2,1,0:T(8,128)(2,1)S(1)}, u32[]{:S(2)}, u32[]{:S(2)}) collective-permute-start(bf16[4,2,128,128]{3,2,1,0:T(8,128)(2,1)S(1)} %slice.6), channel_id=1, source_target_pairs={{0,4},{1,33},{4,8},{5,37},{8,12},{9,41},{12,0},{13,45},{2,6},{3,35... | collective-permute-start | bytes 786440 | tf_op jit(solution)/shard_map/ppermute | solution.py:33
  36.5 8.6 %collective-permute-start.14 = (bf16[4,2,128,128]{3,2,1,0:T(8,128)(2,1)S(1)}, bf16[4,2,128,128]{3,2,1,0:T(8,128)(2,1)S(1)}, u32[]{:S(2)}, u32[]{:S(2)}) collective-permute-start(bf16[4,2,128,128]{3,2,1,0:T(8,128)(2,1)S(1)} %slice.7), channel_id=1, source_target_pairs={{0,12},{1,97},{4,0},{5,101},{8,4},{9,105},{12,8},{13,109},{2,14},{... | collective-permute-start | bytes 786440 | tf_op jit(solution)/shard_map/ppermute | solution.py:33
  45.1 5.3 %collective-permute-start.15 = (bf16[8,2,128,128]{3,2,1,0:T(8,128)(2,1)S(1)}, bf16[8,2,128,128]{3,2,1,0:T(8,128)(2,1)S(1)}, u32[]{:S(2)}, u32[]{:S(2)}) collective-permute-start(bf16[8,2,128,128]{3,2,1,0:T(8,128)(2,1)S(1)} %constant_dynamic-update-slice_fusion.refs_6_.refs_17_), channel_id=1, source_target_pairs={{0,1},{1,0},{4,5},{5,4},{8,9},{9,8},{12,13},{13,12},{2,3},{3,2},{6... | collective-permute-start | bytes 1572872 | tf_op jit(solution)/shard_map/ppermute | solution.py:33

commit v2 on v1

--- a/solution.py
+++ b/solution.py
@@ -116,6 +116,15 @@
     return fold_rows(weights), added
 
 
+def weigh_pair(keys, q_ref, h, values_t, shown=None):
+    queries = jnp.concatenate([q_ref[:, (h + i) * HD : (h + i + 1) * HD] for i in range(2)])
+    if shown is not None:
+        shown = jnp.concatenate([shown, shown], 1)
+    sums, accs = weigh(keys, queries, values_t, shown)
+    for i in range(2):
+        yield h + i, sums[:, i * ROWS : (i + 1) * ROWS], accs[:, i * ROWS : (i + 1) * ROWS]
+
+
 def over_heads(one_head):
     def some(step, unused):
         for h in range(STEP_HEADS):
@@ -224,7 +233,7 @@
         acc_ref[...] = acc_in[...]
 
 
-def prompt_part(q_ref, acc_in, sum_in, held, out_ref, kb, vt, seen, acc, total, top):
+def prompt_part(q_ref, acc_in, sum_in, held, out_ref, put, kb, vt, seen, acc, total, top):
     y = coordinates()[0]
 
     def queries(h):
@@ -233,10 +242,10 @@
     @pl.when(y >= 2)
     def _():
         load_chunk(1, held[3], held[CHUNKS + 3], kb, vt)
-        for h in range(HALF_HEADS):
-            sums, accs = weigh(kb[...], queries(h), vt[...])
-            total[h] = sum_in[h] + sums
-            acc[h] = acc_in[h] + accs
+        for pair in range(0, HALF_HEADS, 2):
+            for h, sums, accs in weigh_pair(kb[...], q_ref, pair, vt[...]):
+                total[h] = sum_in[h] + sums
+                acc[h] = acc_in[h] + accs
 
     @pl.when(y < 2)
     def _():
@@ -252,9 +261,9 @@
         sums = jnp.sum(total[h], axis=0, keepdims=True)
         store(h, sums)
         low, high = jnp.minimum(low, sums), jnp.maximum(high, sums)
-
-    @pl.when(jnp.logical_not(in_range(low, high)))
-    def _():
+    put.start()
+
+    def exact_rows():
         load_chunk(1, held[0], held[CHUNKS], kb, vt)
         for rows, visible in own_pair_seen():
             seen[rows, :] = jnp.where(visible, 1.0, 0.0)
@@ -288,38 +297,51 @@
         lax.fori_loop(0, y, one_pair, 0)
         for h in range(HALF_HEADS):
             store(h, total[h, 0:1])
+        put.start()
+        put.wait()
+
+    return low, high, exact_rows
 
 
 def last_kernel(q_ref, acc_in, sum_in, live_ref, *refs):
     q_rows, acc_rows, sum_rows = refs[:3]
     rows_held, (k_own, v_own, seen_own), refs = refs[3 : 3 + 2 * CHUNKS], refs[11:14], refs[14:]
     held, refs = refs[: 2 * CHUNKS], refs[2 * CHUNKS :]
-    out_ref, out_rows, kb, vt, low, high, block, own = refs[:8]
-    prompt_part(q_rows, acc_rows, sum_rows, rows_held, out_rows, *refs[8:])
+    out_hbm, rows_hbm, out_ref, out_rows, done, kb, vt, low, high, block, own = refs[:11]
+    put_rows = pltpu.make_async_copy(out_rows, rows_hbm, done.at[GROUP])
+    low[...], high[...], exact_rows = prompt_part(
+        q_rows, acc_rows, sum_rows, rows_held, out_rows, put_rows, *refs[11:]
+    )
+
+    def put(h, cols):
+        return pltpu.make_async_copy(out_ref.at[:, cols], out_hbm.at[:, cols], done.at[h])
+
     is_first = coordinates()[3] == 0
     load_chunk(0, rows_held[CHUNKS - 1], rows_held[2 * CHUNKS - 1], kb, vt)
-    low[...] = jnp.full_like(low, 1.0)
-    high[...] = jnp.full_like(high, 1.0)
     live = live_ref[0:1] > 0.5
 
     def store(cols, acc, total):
         shown = jnp.where(live, acc * (1.0 / total), 0.0)
         out_ref[:, cols] = shown.astype(jnp.bfloat16).T
 
-    def one_head(h, cols):
-        sums, accs = weigh(kb[...], q_ref[:, cols], vt[...])
-        total = jnp.sum(sum_in[h] + sums, axis=0, keepdims=True)
-        low[...] = jnp.minimum(low[...], total)
-        high[...] = jnp.maximum(high[...], total)
-        store(cols, acc_in[h] + accs, total)
-
-    over_heads(one_head)
+    for pair in range(0, GROUP, 2):
+        for h, sums, accs in weigh_pair(kb[...], q_ref, pair, vt[...]):
+            total = jnp.sum(sum_in[h] + sums, axis=0, keepdims=True)
+            low[...] = jnp.minimum(low[...], total)
+            high[...] = jnp.maximum(high[...], total)
+            cols = slice(h * HD, (h + 1) * HD)
+            store(cols, acc_in[h] + accs, total)
+            put(h, cols).start()
+    put_rows.wait()
+    for h in range(GROUP):
+        put(h, slice(h * HD, (h + 1) * HD)).wait()
 
     @pl.when(jnp.logical_not(in_range(low[...], high[...])))
     def _():
         pltpu.sync_copy(k_own, own.at[0])
         pltpu.sync_copy(v_own, own.at[1])
-        seen_buf = refs[10].at[:ROWS]
+        exact_rows()
+        seen_buf = refs[13].at[:ROWS]
         pltpu.sync_copy(seen_own, seen_buf)
 
         def exact_head(h, unused):
@@ -345,6 +367,8 @@
             visible = seen_buf[...] > -1.0
             run_max, run_sum, run_acc = online(carried, own[0], own[1].T, queries, visible)
             store(cols, run_acc, run_sum)
+            put(h, cols).start()
+            put(h, cols).wait()
             return unused
 
         lax.fori_loop(0, GROUP, exact_head, 0)
@@ -366,13 +390,17 @@
 def here_kernel(q_ref, q_rows, acc_in, sum_in, here, other, *refs):
     acc_ref, sum_ref, acc_rows, sum_rows, kb, vt, kb_rows, vt_rows, seen = refs
     load_chunk(0, here, other, kb, vt)
-    add_heads(q_ref, acc_in, sum_in, acc_ref, sum_ref, kb, vt)
     load_chunk(1, here, other, kb_rows, vt_rows)
+    for pair in range(0, GROUP, 2):
+        for h, sums, accs in weigh_pair(kb[...], q_ref, pair, vt[...]):
+            sum_ref[h] = sum_in[h] + sums
+            acc_ref[h] = acc_in[h] + accs
+
     for rows, visible in own_pair_seen():
         seen[rows, :] = jnp.where(visible, 0.0, -jnp.inf)
-    for h in range(HALF_HEADS):
-        queries = q_rows[:, h * HD : (h + 1) * HD]
-        sum_rows[h], acc_rows[h] = weigh(kb_rows[...], queries, vt_rows[...], seen[...])
+    for pair in range(0, HALF_HEADS, 2):
+        for h, sums, accs in weigh_pair(kb_rows[...], q_rows, pair, vt_rows[...], seen[...]):
+            sum_rows[h], acc_rows[h] = sums, accs
 
 
 HALF_HEADS = GROUP // 2
@@ -399,12 +427,12 @@
 KEYS = keys_of(PAIR)
 
 
-def call(kernel, name, in_specs, out_shape, scratch, rows, keys):
+def call(kernel, name, in_specs, out_shape, scratch, rows, keys, out=VMEM):
     single = not isinstance(out_shape, tuple)
     return pl.pallas_call(
         kernel,
         in_specs=in_specs,
-        out_specs=VMEM if single else tuple(VMEM for _ in out_shape),
+        out_specs=out if single else tuple(out for _ in out_shape),
         out_shape=out_shape,
         scratch_shapes=scratch,
         cost_estimate=pl.CostEstimate(
@@ -455,7 +483,12 @@
 
 def attend_last(q, state, live, q_rows, state_rows, held, k_own, v_own, seen):
     specs = [VMEM] * (7 + len(held)) + [ANYWHERE] * (3 + len(held))
-    scratch = KEYS + [
+    scratch = [
+        pltpu.VMEM((ROWS, GROUP * HD), jnp.bfloat16),
+        pltpu.VMEM(q_rows.shape, jnp.bfloat16),
+        pltpu.SemaphoreType.DMA((GROUP + 1,)),
+    ]
+    scratch += KEYS + [
         pltpu.VMEM((1, ROWS), jnp.float32),
         pltpu.VMEM((1, ROWS), jnp.float32),
         pltpu.VMEM((2, HD, HD), jnp.bfloat16),
@@ -471,7 +504,7 @@
         jax.ShapeDtypeStruct((ROWS, GROUP * HD), jnp.bfloat16),
         jax.ShapeDtypeStruct(q_rows.shape, jnp.bfloat16),
     )
-    return call(last_kernel, "last_keys", specs, out, scratch, 2 * GROUP * ROWS, PAIR)(
+    return call(last_kernel, "last_keys", specs, out, scratch, 2 * GROUP * ROWS, PAIR, ANYWHERE)(
         q, *state, live, q_rows, *state_rows, *held, k_own, v_own, seen, *held
     )
 
@@ -505,11 +538,10 @@
     state, rows_state = attend_here(q, q_prompt, state, here, here_o)
     left, right = after((left, right), state[1])
     left_o, right_o = move(left, other_core), move(right, other_core)
-    far_l, far_r = move(left[:4], last_axis(1)), move(right[4:], last_axis(3))
+    far = move(left, last_axis(1))
     sides = (left, left_o, right, right_o)
     state = attend_sides(wide_kernel, "wide_keys", GROUP, q, state, sides)
-    far_l, far_r = after((far_l, far_r), state[1])
-    far = jnp.concatenate([far_l, far_r])
+    far = after(far, state[1])
     far_o = move(far, other_core)
     rows_state = attend_sides(side_kernel, "side_rows", HALF_HEADS, q_prompt, rows_state, sides)
     held = (here, left, right, far, here_o, left_o, right_o, after(far_o, rows_state[1]))

time: 225 us -> 230 us (1.022)
  Pallas kernels: 196 us -> 200 us
    pallas_call x1, Pallas kernels: 174 us -> 180 us  [attend_last(): call(last_kernel, 'last_keys', specs, out, scratch, 2 * GROUP * ROWS, PAI...]
    ppermute x16 -> x15, waiting for transfers between devices: 6.15 us -> 7.54 us  [move(): return lax.ppermute(block, AXES, route)]
    ppermute x16 -> x15, starting transfers between devices: 20.1 us -> 19.3 us  [move(): return lax.ppermute(block, AXES, route)]
  transfers between devices with their start and end apart: 16 -> 15, of which waited for: 6 -> 7; matrix products, arithmetic and copies ran while one was open for 0% -> 0% of each run, Pallas kernels for 10% -> 9%
where the time goes in v2:
time: 230 us
  Pallas kernels  200 us (87%)
  starting transfers between devices  19.3 us (8%)
  waiting for transfers between devices  7.54 us (3%)
    pallas_call x1, Pallas kernels, attend_last(): call(last_kernel, 'last_keys', specs, out, scratch, 2 * GROUP * ROWS, PAI...  180 us
    ppermute x15, starting transfers between devices, move(): return lax.ppermute(block, AXES, route)  19.3 us
    pallas_call x2, Pallas kernels, attend_sides(): call(kernel, name, [VMEM] * 7, state_of(heads), scratch, heads * ROWS, 2...  10.8 us
    ppermute x15, waiting for transfers between devices, move(): return lax.ppermute(block, AXES, route)  7.54 us
    pallas_call x1, Pallas kernels, attend_here(): call(here_kernel, 'here_keys', [VMEM] * 6, out, scratch, 3 * HALF_HEADS *...  5.71 us
  transfers between devices with their start and end apart: 15, of which 7 were waited for; matrix products, arithmetic and copies ran while one was open for 0% of the time, Pallas kernels for 9%

profile of v2, /device:TPU:25, one launch (start us, length us, event | category | flops | bytes accessed | tf_op | source)
XLA Modules:
  0.0 229.8 jit_solution(17892457948196886908)
XLA Ops:
  0.6 0.0 copy-start
  0.6 0.0 copy-start.2
  0.7 0.0 copy-start.3
  0.7 0.0 copy-start.4
  0.7 0.8 collective-permute-start
  1.4 0.1 collective-permute-start.1
  1.5 0.9 pad_maximum_fusion.1.own
  2.4 0.1 collective-permute-done.k_other
  2.5 0.4 collective-permute-done.1.v_other
  2.9 1.3 collective-permute-start.2
  4.2 1.5 collective-permute-start.3
  5.7 1.5 collective-permute-start.4
  7.9 0.0 collective-permute-done.2
  7.9 0.0 collective-permute-done.3
  7.9 2.7 %collective-permute-done.4 = bf16[2,64,256]{2,1,0:T(8,128)(2,1)S(1)} collective-permute-done((bf16[2,64,256]{2,1,0:T(8,128)(2,1)S(1)}, bf16[2,64,256]{2,1,0:T(8,128)(2,1)S(1)}, u32[]{:S(2)}, u32[]{:S(2)}) %collective-permute-start.4) | collective-permute-done | bytes 65568 | tf_op jit(solution)/shard_map/ppermute | solution.py:33
  10.6 0.1 constant_dynamic-slice_fusion
  10.7 1.7 collective-permute-start.5
  12.4 2.2 collective-permute-start.6
  14.6 1.2 collective-permute-start.7
  15.8 0.0 copy-done
  15.8 0.0 copy-done.2
  15.9 0.0 copy-done.3
  15.9 0.0 copy-done.4
  15.9 0.0 copy-start.1
  15.9 4.0 %own_keys.1 = (f32[8,128,512]{2,1,0:T(8,128)S(1)}, f32[8,8,512]{2,1,0:T(8,128)S(1)}, f32[512,512]{1,0:T(8,128)S(1)}, f32[8,512]{1,0:T(8,128)S(1)}) custom-call(s32[1,8]{1,0:T(1,128)S(1)} %copy-done.4, s32[1]{0:T(128)S(6)} %copy.10.len_ref, bf16[512,1024]{1,0:T(8,128)(2,1)S(1)} %bitcast.11, bf16[512,128]{1,0:T(8,128)(2,1)S(1)} %bitcast.15, ...), custom_call_target="tpu_custom_call" | custom-call | flops 2147483648 | bytes 6291456 | tf_op jit(solution)/shard_map/own_keys/pallas_call | solution.py:453
  19.8 0.0 collective-permute-done.5.refs_1_
  19.8 0.0 collective-permute-done.6.refs_2_
  19.8 1.9 collective-permute-done.7.refs_3_
  21.7 0.1 arrange.1.here.refs_3_.refs_14_
  21.9 1.3 collective-permute-start.8
  23.2 0.2 collective-permute-start.10
  23.4 2.5 %collective-permute-start.9 = (bf16[8,2,128,128]{3,2,1,0:T(8,128)(2,1)S(1)}, bf16[8,2,128,128]{3,2,1,0:T(8,128)(2,1)S(1)}, u32[]{:S(2)}, u32[]{:S(2)}) collective-permute-start(bf16[8,2,128,128]{3,2,1,0:T(8,128)(2,1)S(1)} %arrange.1.here.refs_3_.refs_14_), channel_id=1, source_target_pairs={{0,4},{1,33},{4,8},{5,37},{8,12},{9,41},{12,0},{13,45},{2,6},{3,35... | collective-permute-start | bytes 1572872 | tf_op jit(solution)/shard_map/ppermute | solution.py:33
  25.9 0.0 collective-permute-done.8.other.refs_7_.refs_18_
  25.9 0.0 copy-done.1
  25.9 5.7 %here_keys.1 = (f32[8,128,512]{2,1,0:T(8,128)S(1)}, f32[8,8,512]{2,1,0:T(8,128)S(1)}, f32[4,128,512]{2,1,0:T(8,128)S(1)}, f32[4,8,512]{2,1,0:T(8,128)S(1)}) custom-call(bf16[512,1024]{1,0:T(8,128)(2,1)S(1)} %bitcast.12, bf16[512,512]{1,0:T(8,128)(2,1)S(1)} %copy-done.1, f32[8,128,512]{2,1,0:T(8,128)S(1)} %get-tuple-element.34.acc_in, ...), custom_call_target="tpu_custom_call" | custom-call | flops 6442450944 | bytes 6291456 | tf_op jit(solution)/shard_map/here_keys/pallas_call | solution.py:471
  31.6 1.1 collective-permute-done.10.right.refs_5_.refs_16_
  32.7 0.0 collective-permute-done.9.left.refs_4_.refs_15_
  32.7 2.7 %collective-permute-start.11 = (bf16[8,2,128,128]{3,2,1,0:T(8,128)(2,1)S(1)}, bf16[8,2,128,128]{3,2,1,0:T(8,128)(2,1)S(1)}, u32[]{:S(2)}, u32[]{:S(2)}) collective-permute-start(bf16[8,2,128,128]{3,2,1,0:T(8,128)(2,1)S(1)} %collective-permute-done.9.left.refs_4_.refs_15_), channel_id=1, source_target_pairs={{0,1},{1,0},{4,5},{5,4},{8,9},{9,8},{12,13},{13,12},{2,3},{3,2},{6... | collective-permute-start | bytes 1572872 | tf_op jit(solution)/shard_map/ppermute | solution.py:33
  35.4 0.0 collective-permute-start.12
  35.4 1.0 collective-permute-start.13
  36.4 0.6 collective-permute-done.11.left_o.refs_8_.refs_19_
  36.9 0.7 collective-permute-done.12.right_o.refs_9_.refs_20_
  37.7 7.2 %wide_keys.1 = (f32[8,128,512]{2,1,0:T(8,128)S(1)}, f32[8,8,512]{2,1,0:T(8,128)S(1)}) custom-call(bf16[512,1024]{1,0:T(8,128)(2,1)S(1)} %bitcast.13, f32[8,128,512]{2,1,0:T(8,128)S(1)} %get-tuple-element.41.acc_in, f32[8,8,512]{2,1,0:T(8,128)S(1)} %get-tuple-element.42.sum_in, bf16[8,2,128,128]{3,2,1,0:T(8,128)(2,1)S(1)} %collective-permute-done.9.left.refs_4_.refs_15_, ...), custom_call_target="tpu_custom_call" | custom-call | flops 8589934592 | bytes 6291456 | tf_op jit(solution)/shard_map/wide_keys/pallas_call | solution.py:479
  44.9 0.0 collective-permute-done.13.refs_6_.refs_17_
  44.9 1.4 collective-permute-start.14
  46.3 3.6 %side_rows.1 = (f32[4,128,512]{2,1,0:T(8,128)S(1)}, f32[4,8,512]{2,1,0:T(8,128)S(1)}) custom-call(bf16[512,512]{1,0:T(8,128)(2,1)S(1)} %copy-done.1, f32[4,128,512]{2,1,0:T(8,128)S(1)} %get-tuple-element.47.acc_in, f32[4,8,512]{2,1,0:T(8,128)S(1)} %get-tuple-element.48.sum_in, bf16[8,2,128,128]{3,2,1,0:T(8,128)(2,1)S(1)} %collective-permute-done.9.left.refs_4_.refs_15_, ...), custom_call_target="tpu_custom_call" | custom-call | flops 4294967296 | bytes 6291456 | tf_op jit(solution)/shard_map/side_rows/pallas_call | solution.py:479
  50.0 0.0 collective-permute-done.14.refs_10_.refs_21_
  50.0 179.6 %last_keys.1 = (bf16[512,1024]{1,0:T(8,128)(2,1)}, bf16[512,512]{1,0:T(8,128)(2,1)}) custom-call(bf16[512,1024]{1,0:T(8,128)(2,1)S(1)} %bitcast.14, f32[8,128,512]{2,1,0:T(8,128)S(1)} %get-tuple-element.45.acc_in, f32[8,8,512]{2,1,0:T(8,128)S(1)} %get-tuple-element.46.sum_in, f32[8,512]{1,0:T(8,128)S(1)} %get-tuple-element.36.live_ref, ...), custom_call_target="tpu_custom_call" | custom-call | flops 8589934592 | bytes 6291456 | tf_op jit(solution)/shard_map/last_keys/pallas_call | solution.py:507
  (2 shorter events, 0.1 us)
Async XLA Ops:
  0.6 15.2 %copy-start = (bf16[1,512,1024]{2,1,0:T(8,128)(2,1)S(1)}, bf16[1,512,1024]{2,1,0:T(8,128)(2,1)}, u32[]{:S(2)}) copy-start(bf16[1,512,1024]{2,1,0:T(8,128)(2,1)} %param.11) | copy-start | bytes 3145732
  0.6 15.2 %copy-start.2 = (bf16[1,512,128]{2,1,0:T(8,128)(2,1)S(1)}, bf16[1,512,128]{2,1,0:T(8,128)(2,1)}, u32[]{:S(2)}) copy-start(bf16[1,512,128]{2,1,0:T(8,128)(2,1)} %param.12) | copy-start | bytes 393220
  0.7 15.2 %copy-start.3 = (bf16[1,512,128]{2,1,0:T(8,128)(2,1)S(1)}, bf16[1,512,128]{2,1,0:T(8,128)(2,1)}, u32[]{:S(2)}) copy-start(bf16[1,512,128]{2,1,0:T(8,128)(2,1)} %param.13) | copy-start | bytes 393220
  0.7 15.2 %copy-start.4 = (s32[1,8]{1,0:T(1,128)S(1)}, s32[1,8]{1,0:T(1,128)}, u32[]{:S(2)}) copy-start(s32[1,8]{1,0:T(1,128)} %tree_ref.1) | copy-start | bytes 100
  0.7 1.9 collective-permute-start
  1.4 1.5 collective-permute-start.1
  2.9 4.9 %collective-permute-start.2 = (bf16[2,64,256]{2,1,0:T(8,128)(2,1)S(1)}, bf16[2,64,256]{2,1,0:T(8,128)(2,1)S(1)}, u32[]{:S(2)}, u32[]{:S(2)}) collective-permute-start(bf16[2,64,256]{2,1,0:T(8,128)(2,1)S(1)} %get-tuple-element.30), channel_id=1, source_target_pairs={{0,32},{1,5},{4,36},{5,9},{8,40},{9,13},{12,44},{13,1},{2,34},{3,7... | collective-permute-start | bytes 196616 | tf_op jit(solution)/shard_map/ppermute | solution.py:33
  4.2 3.7 %collective-permute-start.3 = (bf16[2,64,256]{2,1,0:T(8,128)(2,1)S(1)}, bf16[2,64,256]{2,1,0:T(8,128)(2,1)S(1)}, u32[]{:S(2)}, u32[]{:S(2)}) collective-permute-start(bf16[2,64,256]{2,1,0:T(8,128)(2,1)S(1)} %get-tuple-element.31), channel_id=1, source_target_pairs={{0,96},{1,13},{4,100},{5,1},{8,104},{9,5},{12,108},{13,9},{2,98},{... | collective-permute-start | bytes 196616 | tf_op jit(solution)/shard_map/ppermute | solution.py:33
  5.7 4.9 %collective-permute-start.4 = (bf16[2,64,256]{2,1,0:T(8,128)(2,1)S(1)}, bf16[2,64,256]{2,1,0:T(8,128)(2,1)S(1)}, u32[]{:S(2)}, u32[]{:S(2)}) collective-permute-start(bf16[2,64,256]{2,1,0:T(8,128)(2,1)S(1)} %get-tuple-element.32), channel_id=1, source_target_pairs={{0,64},{1,9},{4,68},{5,13},{8,72},{9,1},{12,76},{13,5},{2,66},{3,1... | collective-permute-start | bytes 196616 | tf_op jit(solution)/shard_map/ppermute | solution.py:33
  10.7 9.1 %collective-permute-start.5 = (bf16[4,2,64,128]{3,2,1,0:T(8,128)(2,1)S(1)}, bf16[4,2,64,128]{3,2,1,0:T(8,128)(2,1)S(1)}, u32[]{:S(2)}, u32[]{:S(2)}) collective-permute-start(bf16[4,2,64,128]{3,2,1,0:T(8,128)(2,1)S(1)} %get-tuple-element.58), channel_id=1, source_target_pairs={{0,2},{1,3},{4,6},{5,7},{8,10},{9,11},{12,14},{13,15},{2,16},{3,17... | collective-permute-start | bytes 393224 | tf_op jit(solution)/shard_map/ppermute | solution.py:33
  12.4 7.4 %collective-permute-start.6 = (bf16[4,2,64,128]{3,2,1,0:T(8,128)(2,1)S(1)}, bf16[4,2,64,128]{3,2,1,0:T(8,128)(2,1)S(1)}, u32[]{:S(2)}, u32[]{:S(2)}) collective-permute-start(bf16[4,2,64,128]{3,2,1,0:T(8,128)(2,1)S(1)} %get-tuple-element.57), channel_id=1, source_target_pairs={{0,18},{1,19},{4,22},{5,23},{8,26},{9,27},{12,30},{13,31},{2,0},{3... | collective-permute-start | bytes 393224 | tf_op jit(solution)/shard_map/ppermute | solution.py:33
  14.6 7.1 %collective-permute-start.7 = (bf16[4,2,64,128]{3,2,1,0:T(8,128)(2,1)S(1)}, bf16[4,2,64,128]{3,2,1,0:T(8,128)(2,1)S(1)}, u32[]{:S(2)}, u32[]{:S(2)}) collective-permute-start(bf16[4,2,64,128]{3,2,1,0:T(8,128)(2,1)S(1)} %get-tuple-element.56), channel_id=1, source_target_pairs={{0,16},{1,17},{4,20},{5,21},{8,24},{9,25},{12,28},{13,29},{2,18},{... | collective-permute-start | bytes 393224 | tf_op jit(solution)/shard_map/ppermute | solution.py:33
  15.9 10.0 %copy-start.1 = (bf16[512,512]{1,0:T(8,128)(2,1)S(1)}, bf16[512,512]{1,0:T(8,128)(2,1)}, u32[]{:S(2)}) copy-start(bf16[512,512]{1,0:T(8,128)(2,1)} %refs_0_.1) | copy-start | bytes 1572868
  21.9 4.0 %collective-permute-start.8 = (bf16[8,2,128,128]{3,2,1,0:T(8,128)(2,1)S(1)}, bf16[8,2,128,128]{3,2,1,0:T(8,128)(2,1)S(1)}, u32[]{:S(2)}, u32[]{:S(2)}) collective-permute-start(bf16[8,2,128,128]{3,2,1,0:T(8,128)(2,1)S(1)} %arrange.1.here.refs_3_.refs_14_), channel_id=1, source_target_pairs={{0,1},{1,0},{4,5},{5,4},{8,9},{9,8},{12,13},{13,12},{2,3},{3,2},{6... | collective-permute-start | bytes 1572872 | tf_op jit(solution)/shard_map/ppermute | solution.py:33
  23.2 9.5 %collective-permute-start.10 = (bf16[8,2,128,128]{3,2,1,0:T(8,128)(2,1)S(1)}, bf16[8,2,128,128]{3,2,1,0:T(8,128)(2,1)S(1)}, u32[]{:S(2)}, u32[]{:S(2)}) collective-permute-start(bf16[8,2,128,128]{3,2,1,0:T(8,128)(2,1)S(1)} %arrange.1.here.refs_3_.refs_14_), channel_id=1, source_target_pairs={{0,12},{1,97},{4,0},{5,101},{8,4},{9,105},{12,8},{13,109},{2,14},{... | collective-permute-start | bytes 1572872 | tf_op jit(solution)/shard_map/ppermute | solution.py:33
  23.4 9.3 %collective-permute-start.9 = (bf16[8,2,128,128]{3,2,1,0:T(8,128)(2,1)S(1)}, bf16[8,2,128,128]{3,2,1,0:T(8,128)(2,1)S(1)}, u32[]{:S(2)}, u32[]{:S(2)}) collective-permute-start(bf16[8,2,128,128]{3,2,1,0:T(8,128)(2,1)S(1)} %arrange.1.here.refs_3_.refs_14_), channel_id=1, source_target_pairs={{0,4},{1,33},{4,8},{5,37},{8,12},{9,41},{12,0},{13,45},{2,6},{3,35... | collective-permute-start | bytes 1572872 | tf_op jit(solution)/shard_map/ppermute | solution.py:33
  32.7 4.2 %collective-permute-start.11 = (bf16[8,2,128,128]{3,2,1,0:T(8,128)(2,1)S(1)}, bf16[8,2,128,128]{3,2,1,0:T(8,128)(2,1)S(1)}, u32[]{:S(2)}, u32[]{:S(2)}) collective-permute-start(bf16[8,2,128,128]{3,2,1,0:T(8,128)(2,1)S(1)} %collective-permute-done.9.left.refs_4_.refs_15_), channel_id=1, source_target_pairs={{0,1},{1,0},{4,5},{5,4},{8,9},{9,8},{12,13},{13,12},{2,3},{3,2},{6... | collective-permute-start | bytes 1572872 | tf_op jit(solution)/shard_map/ppermute | solution.py:33
  35.4 2.3 collective-permute-start.12
  35.4 9.5 %collective-permute-start.13 = (bf16[8,2,128,128]{3,2,1,0:T(8,128)(2,1)S(1)}, bf16[8,2,128,128]{3,2,1,0:T(8,128)(2,1)S(1)}, u32[]{:S(2)}, u32[]{:S(2)}) collective-permute-start(bf16[8,2,128,128]{3,2,1,0:T(8,128)(2,1)S(1)} %collective-permute-done.9.left.refs_4_.refs_15_), channel_id=1, source_target_pairs={{0,4},{1,33},{4,8},{5,37},{8,12},{9,41},{12,0},{13,45},{2,6},{3,35... | collective-permute-start | bytes 1572872 | tf_op jit(solution)/shard_map/ppermute | solution.py:33
  44.9 5.1 %collective-permute-start.14 = (bf16[8,2,128,128]{3,2,1,0:T(8,128)(2,1)S(1)}, bf16[8,2,128,128]{3,2,1,0:T(8,128)(2,1)S(1)}, u32[]{:S(2)}, u32[]{:S(2)}) collective-permute-start(bf16[8,2,128,128]{3,2,1,0:T(8,128)(2,1)S(1)} %collective-permute-done.13.refs_6_.refs_17_), channel_id=1, source_target_pairs={{0,1},{1,0},{4,5},{5,4},{8,9},{9,8},{12,13},{13,12},{2,3},{3,2},{6... | collective-permute-start | bytes 1572872 | tf_op jit(solution)/shard_map/ppermute | solution.py:33

commit v3 on v2

--- a/solution.py
+++ b/solution.py
@@ -332,11 +332,12 @@
             cols = slice(h * HD, (h + 1) * HD)
             store(cols, acc_in[h] + accs, total)
             put(h, cols).start()
+    good = in_range(low[...], high[...])
     put_rows.wait()
     for h in range(GROUP):
         put(h, slice(h * HD, (h + 1) * HD)).wait()
 
-    @pl.when(jnp.logical_not(in_range(low[...], high[...])))
+    @pl.when(jnp.logical_not(good))
     def _():
         pltpu.sync_copy(k_own, own.at[0])
         pltpu.sync_copy(v_own, own.at[1])
@@ -468,7 +469,7 @@
 def attend_here(q, q_rows, state, here, other):
     scratch = KEYS + KEYS + [pltpu.VMEM((PAIR, ROWS), jnp.float32)]
     out = state_of(GROUP) + state_of(HALF_HEADS)
-    outs = call(here_kernel, "here_keys", [VMEM] * 6, out, scratch, 3 * HALF_HEADS * ROWS, PAIR)(
+    outs = call(here_kernel, "here_keys", [VMEM] * 6, out, scratch, 8, 8)(
         q, q_rows, *state, here, other
     )
     return outs[:2], outs[2:]

time: 230 us -> 230 us (level)
  no operation moved by 1% of the time
where the time goes in v3:
time: 230 us
  Pallas kernels  200 us (87%)
  starting transfers between devices  19.3 us (8%)
  waiting for transfers between devices  7.53 us (3%)
    pallas_call x1, Pallas kernels, attend_last(): call(last_kernel, 'last_keys', specs, out, scratch, 2 * GROUP * ROWS, PAI...  179 us
    ppermute x15, starting transfers between devices, move(): return lax.ppermute(block, AXES, route)  19.3 us
    pallas_call x2, Pallas kernels, attend_sides(): call(kernel, name, [VMEM] * 7, state_of(heads), scratch, heads * ROWS, 2...  10.8 us
    ppermute x15, waiting for transfers between devices, move(): return lax.ppermute(block, AXES, route)  7.53 us
    pallas_call x1, Pallas kernels, attend_here(): call(here_kernel, 'here_keys', [VMEM] * 6, out, scratch, 8, 8)  5.72 us
  transfers between devices with their start and end apart: 15, of which 7 were waited for; matrix products, arithmetic and copies ran while one was open for 0% of the time, Pallas kernels for 9%

profile of v3, /device:TPU:25, one launch (start us, length us, event | category | flops | bytes accessed | tf_op | source)
XLA Modules:
  0.0 229.6 jit_solution(951557619526562616)
XLA Ops:
  0.6 0.0 copy-start
  0.6 0.0 copy-start.2
  0.7 0.0 copy-start.3
  0.7 0.0 copy-start.4
  0.7 0.8 collective-permute-start
  1.4 0.1 collective-permute-start.1
  1.5 0.9 pad_maximum_fusion.1.own
  2.4 0.1 collective-permute-done.k_other
  2.5 0.4 collective-permute-done.1.v_other
  2.9 1.3 collective-permute-start.2
  4.2 1.5 collective-permute-start.3
  5.7 1.5 collective-permute-start.4
  7.9 0.0 collective-permute-done.2
  7.9 0.0 collective-permute-done.3
  7.9 2.7 %collective-permute-done.4 = bf16[2,64,256]{2,1,0:T(8,128)(2,1)S(1)} collective-permute-done((bf16[2,64,256]{2,1,0:T(8,128)(2,1)S(1)}, bf16[2,64,256]{2,1,0:T(8,128)(2,1)S(1)}, u32[]{:S(2)}, u32[]{:S(2)}) %collective-permute-start.4) | collective-permute-done | bytes 65568 | tf_op jit(solution)/shard_map/ppermute | solution.py:33
  10.6 0.1 constant_dynamic-slice_fusion
  10.7 1.7 collective-permute-start.5
  12.4 2.2 collective-permute-start.6
  14.6 1.2 collective-permute-start.7
  15.8 0.0 copy-done
  15.8 0.0 copy-done.2
  15.9 0.0 copy-done.3
  15.9 0.0 copy-done.4
  15.9 0.0 copy-start.1
  15.9 4.0 %own_keys.1 = (f32[8,128,512]{2,1,0:T(8,128)S(1)}, f32[8,8,512]{2,1,0:T(8,128)S(1)}, f32[512,512]{1,0:T(8,128)S(1)}, f32[8,512]{1,0:T(8,128)S(1)}) custom-call(s32[1,8]{1,0:T(1,128)S(1)} %copy-done.4, s32[1]{0:T(128)S(6)} %copy.10.len_ref, bf16[512,1024]{1,0:T(8,128)(2,1)S(1)} %bitcast.10, bf16[512,128]{1,0:T(8,128)(2,1)S(1)} %bitcast.15, ...), custom_call_target="tpu_custom_call" | custom-call | flops 2147483648 | bytes 6291456 | tf_op jit(solution)/shard_map/own_keys/pallas_call | solution.py:454
  19.8 0.0 collective-permute-done.5.refs_1_
  19.8 0.0 collective-permute-done.6.refs_2_
  19.8 1.9 collective-permute-done.7.refs_3_
  21.7 0.1 arrange.1.here.refs_3_.refs_14_
  21.9 1.3 collective-permute-start.8
  23.2 0.2 collective-permute-start.10
  23.4 2.5 %collective-permute-start.9 = (bf16[8,2,128,128]{3,2,1,0:T(8,128)(2,1)S(1)}, bf16[8,2,128,128]{3,2,1,0:T(8,128)(2,1)S(1)}, u32[]{:S(2)}, u32[]{:S(2)}) collective-permute-start(bf16[8,2,128,128]{3,2,1,0:T(8,128)(2,1)S(1)} %arrange.1.here.refs_3_.refs_14_), channel_id=1, source_target_pairs={{0,4},{1,33},{4,8},{5,37},{8,12},{9,41},{12,0},{13,45},{2,6},{3,35... | collective-permute-start | bytes 1572872 | tf_op jit(solution)/shard_map/ppermute | solution.py:33
  25.9 0.0 collective-permute-done.8.other.refs_7_.refs_18_
  25.9 0.0 copy-done.1
  25.9 5.7 %here_keys.1 = (f32[8,128,512]{2,1,0:T(8,128)S(1)}, f32[8,8,512]{2,1,0:T(8,128)S(1)}, f32[4,128,512]{2,1,0:T(8,128)S(1)}, f32[4,8,512]{2,1,0:T(8,128)S(1)}) custom-call(bf16[512,1024]{1,0:T(8,128)(2,1)S(1)} %bitcast.11, bf16[512,512]{1,0:T(8,128)(2,1)S(1)} %copy-done.1, f32[8,128,512]{2,1,0:T(8,128)S(1)} %get-tuple-element.34.acc_in, ...), custom_call_target="tpu_custom_call" | custom-call | flops 65536 | bytes 6291456 | tf_op jit(solution)/shard_map/here_keys/pallas_call | solution.py:472
  31.6 1.1 collective-permute-done.10.right.refs_5_.refs_16_
  32.7 0.0 collective-permute-done.9.left.refs_4_.refs_15_
  32.7 2.7 %collective-permute-start.11 = (bf16[8,2,128,128]{3,2,1,0:T(8,128)(2,1)S(1)}, bf16[8,2,128,128]{3,2,1,0:T(8,128)(2,1)S(1)}, u32[]{:S(2)}, u32[]{:S(2)}) collective-permute-start(bf16[8,2,128,128]{3,2,1,0:T(8,128)(2,1)S(1)} %collective-permute-done.9.left.refs_4_.refs_15_), channel_id=1, source_target_pairs={{0,1},{1,0},{4,5},{5,4},{8,9},{9,8},{12,13},{13,12},{2,3},{3,2},{6... | collective-permute-start | bytes 1572872 | tf_op jit(solution)/shard_map/ppermute | solution.py:33
  35.4 0.0 collective-permute-start.12
  35.4 1.0 collective-permute-start.13
  36.4 0.6 collective-permute-done.11.left_o.refs_8_.refs_19_
  36.9 0.7 collective-permute-done.12.right_o.refs_9_.refs_20_
  37.7 7.2 %wide_keys.1 = (f32[8,128,512]{2,1,0:T(8,128)S(1)}, f32[8,8,512]{2,1,0:T(8,128)S(1)}) custom-call(bf16[512,1024]{1,0:T(8,128)(2,1)S(1)} %bitcast.12, f32[8,128,512]{2,1,0:T(8,128)S(1)} %get-tuple-element.41.acc_in, f32[8,8,512]{2,1,0:T(8,128)S(1)} %get-tuple-element.42.sum_in, bf16[8,2,128,128]{3,2,1,0:T(8,128)(2,1)S(1)} %collective-permute-done.9.left.refs_4_.refs_15_, ...), custom_call_target="tpu_custom_call" | custom-call | flops 8589934592 | bytes 6291456 | tf_op jit(solution)/shard_map/wide_keys/pallas_call | solution.py:480
  44.9 0.0 collective-permute-done.13.refs_6_.refs_17_
  44.9 1.4 collective-permute-start.14
  46.3 3.6 %side_rows.1 = (f32[4,128,512]{2,1,0:T(8,128)S(1)}, f32[4,8,512]{2,1,0:T(8,128)S(1)}) custom-call(bf16[512,512]{1,0:T(8,128)(2,1)S(1)} %copy-done.1, f32[4,128,512]{2,1,0:T(8,128)S(1)} %get-tuple-element.47.acc_in, f32[4,8,512]{2,1,0:T(8,128)S(1)} %get-tuple-element.48.sum_in, bf16[8,2,128,128]{3,2,1,0:T(8,128)(2,1)S(1)} %collective-permute-done.9.left.refs_4_.refs_15_, ...), custom_call_target="tpu_custom_call" | custom-call | flops 4294967296 | bytes 6291456 | tf_op jit(solution)/shard_map/side_rows/pallas_call | solution.py:480
  50.0 0.0 collective-permute-done.14.refs_10_.refs_21_
  50.0 179.4 %last_keys.1 = (bf16[512,1024]{1,0:T(8,128)(2,1)}, bf16[512,512]{1,0:T(8,128)(2,1)}) custom-call(bf16[512,1024]{1,0:T(8,128)(2,1)S(1)} %bitcast.13, f32[8,128,512]{2,1,0:T(8,128)S(1)} %get-tuple-element.45.acc_in, f32[8,8,512]{2,1,0:T(8,128)S(1)} %get-tuple-element.46.sum_in, f32[8,512]{1,0:T(8,128)S(1)} %get-tuple-element.36.live_ref, ...), custom_call_target="tpu_custom_call" | custom-call | flops 8589934592 | bytes 6291456 | tf_op jit(solution)/shard_map/last_keys/pallas_call | solution.py:508
  (2 shorter events, 0.1 us)
Async XLA Ops:
  0.6 15.2 %copy-start = (bf16[1,512,1024]{2,1,0:T(8,128)(2,1)S(1)}, bf16[1,512,1024]{2,1,0:T(8,128)(2,1)}, u32[]{:S(2)}) copy-start(bf16[1,512,1024]{2,1,0:T(8,128)(2,1)} %param.11) | copy-start | bytes 3145732
  0.6 15.2 %copy-start.2 = (bf16[1,512,128]{2,1,0:T(8,128)(2,1)S(1)}, bf16[1,512,128]{2,1,0:T(8,128)(2,1)}, u32[]{:S(2)}) copy-start(bf16[1,512,128]{2,1,0:T(8,128)(2,1)} %param.12) | copy-start | bytes 393220
  0.7 15.2 %copy-start.3 = (bf16[1,512,128]{2,1,0:T(8,128)(2,1)S(1)}, bf16[1,512,128]{2,1,0:T(8,128)(2,1)}, u32[]{:S(2)}) copy-start(bf16[1,512,128]{2,1,0:T(8,128)(2,1)} %param.13) | copy-start | bytes 393220
  0.7 15.2 %copy-start.4 = (s32[1,8]{1,0:T(1,128)S(1)}, s32[1,8]{1,0:T(1,128)}, u32[]{:S(2)}) copy-start(s32[1,8]{1,0:T(1,128)} %tree_ref.1) | copy-start | bytes 100
  0.7 1.9 collective-permute-start
  1.4 1.5 collective-permute-start.1
  2.9 4.9 %collective-permute-start.2 = (bf16[2,64,256]{2,1,0:T(8,128)(2,1)S(1)}, bf16[2,64,256]{2,1,0:T(8,128)(2,1)S(1)}, u32[]{:S(2)}, u32[]{:S(2)}) collective-permute-start(bf16[2,64,256]{2,1,0:T(8,128)(2,1)S(1)} %get-tuple-element.30), channel_id=1, source_target_pairs={{0,32},{1,5},{4,36},{5,9},{8,40},{9,13},{12,44},{13,1},{2,34},{3,7... | collective-permute-start | bytes 196616 | tf_op jit(solution)/shard_map/ppermute | solution.py:33
  4.2 3.7 %collective-permute-start.3 = (bf16[2,64,256]{2,1,0:T(8,128)(2,1)S(1)}, bf16[2,64,256]{2,1,0:T(8,128)(2,1)S(1)}, u32[]{:S(2)}, u32[]{:S(2)}) collective-permute-start(bf16[2,64,256]{2,1,0:T(8,128)(2,1)S(1)} %get-tuple-element.31), channel_id=1, source_target_pairs={{0,96},{1,13},{4,100},{5,1},{8,104},{9,5},{12,108},{13,9},{2,98},{... | collective-permute-start | bytes 196616 | tf_op jit(solution)/shard_map/ppermute | solution.py:33
  5.7 4.9 %collective-permute-start.4 = (bf16[2,64,256]{2,1,0:T(8,128)(2,1)S(1)}, bf16[2,64,256]{2,1,0:T(8,128)(2,1)S(1)}, u32[]{:S(2)}, u32[]{:S(2)}) collective-permute-start(bf16[2,64,256]{2,1,0:T(8,128)(2,1)S(1)} %get-tuple-element.32), channel_id=1, source_target_pairs={{0,64},{1,9},{4,68},{5,13},{8,72},{9,1},{12,76},{13,5},{2,66},{3,1... | collective-permute-start | bytes 196616 | tf_op jit(solution)/shard_map/ppermute | solution.py:33
  10.7 9.1 %collective-permute-start.5 = (bf16[4,2,64,128]{3,2,1,0:T(8,128)(2,1)S(1)}, bf16[4,2,64,128]{3,2,1,0:T(8,128)(2,1)S(1)}, u32[]{:S(2)}, u32[]{:S(2)}) collective-permute-start(bf16[4,2,64,128]{3,2,1,0:T(8,128)(2,1)S(1)} %get-tuple-element.58), channel_id=1, source_target_pairs={{0,2},{1,3},{4,6},{5,7},{8,10},{9,11},{12,14},{13,15},{2,16},{3,17... | collective-permute-start | bytes 393224 | tf_op jit(solution)/shard_map/ppermute | solution.py:33
  12.4 7.4 %collective-permute-start.6 = (bf16[4,2,64,128]{3,2,1,0:T(8,128)(2,1)S(1)}, bf16[4,2,64,128]{3,2,1,0:T(8,128)(2,1)S(1)}, u32[]{:S(2)}, u32[]{:S(2)}) collective-permute-start(bf16[4,2,64,128]{3,2,1,0:T(8,128)(2,1)S(1)} %get-tuple-element.57), channel_id=1, source_target_pairs={{0,18},{1,19},{4,22},{5,23},{8,26},{9,27},{12,30},{13,31},{2,0},{3... | collective-permute-start | bytes 393224 | tf_op jit(solution)/shard_map/ppermute | solution.py:33
  14.6 7.1 %collective-permute-start.7 = (bf16[4,2,64,128]{3,2,1,0:T(8,128)(2,1)S(1)}, bf16[4,2,64,128]{3,2,1,0:T(8,128)(2,1)S(1)}, u32[]{:S(2)}, u32[]{:S(2)}) collective-permute-start(bf16[4,2,64,128]{3,2,1,0:T(8,128)(2,1)S(1)} %get-tuple-element.56), channel_id=1, source_target_pairs={{0,16},{1,17},{4,20},{5,21},{8,24},{9,25},{12,28},{13,29},{2,18},{... | collective-permute-start | bytes 393224 | tf_op jit(solution)/shard_map/ppermute | solution.py:33
  15.9 10.0 %copy-start.1 = (bf16[512,512]{1,0:T(8,128)(2,1)S(1)}, bf16[512,512]{1,0:T(8,128)(2,1)}, u32[]{:S(2)}) copy-start(bf16[512,512]{1,0:T(8,128)(2,1)} %refs_0_.1) | copy-start | bytes 1572868
  21.9 4.0 %collective-permute-start.8 = (bf16[8,2,128,128]{3,2,1,0:T(8,128)(2,1)S(1)}, bf16[8,2,128,128]{3,2,1,0:T(8,128)(2,1)S(1)}, u32[]{:S(2)}, u32[]{:S(2)}) collective-permute-start(bf16[8,2,128,128]{3,2,1,0:T(8,128)(2,1)S(1)} %arrange.1.here.refs_3_.refs_14_), channel_id=1, source_target_pairs={{0,1},{1,0},{4,5},{5,4},{8,9},{9,8},{12,13},{13,12},{2,3},{3,2},{6... | collective-permute-start | bytes 1572872 | tf_op jit(solution)/shard_map/ppermute | solution.py:33
  23.2 9.5 %collective-permute-start.10 = (bf16[8,2,128,128]{3,2,1,0:T(8,128)(2,1)S(1)}, bf16[8,2,128,128]{3,2,1,0:T(8,128)(2,1)S(1)}, u32[]{:S(2)}, u32[]{:S(2)}) collective-permute-start(bf16[8,2,128,128]{3,2,1,0:T(8,128)(2,1)S(1)} %arrange.1.here.refs_3_.refs_14_), channel_id=1, source_target_pairs={{0,12},{1,97},{4,0},{5,101},{8,4},{9,105},{12,8},{13,109},{2,14},{... | collective-permute-start | bytes 1572872 | tf_op jit(solution)/shard_map/ppermute | solution.py:33
  23.4 9.3 %collective-permute-start.9 = (bf16[8,2,128,128]{3,2,1,0:T(8,128)(2,1)S(1)}, bf16[8,2,128,128]{3,2,1,0:T(8,128)(2,1)S(1)}, u32[]{:S(2)}, u32[]{:S(2)}) collective-permute-start(bf16[8,2,128,128]{3,2,1,0:T(8,128)(2,1)S(1)} %arrange.1.here.refs_3_.refs_14_), channel_id=1, source_target_pairs={{0,4},{1,33},{4,8},{5,37},{8,12},{9,41},{12,0},{13,45},{2,6},{3,35... | collective-permute-start | bytes 1572872 | tf_op jit(solution)/shard_map/ppermute | solution.py:33
  32.7 4.2 %collective-permute-start.11 = (bf16[8,2,128,128]{3,2,1,0:T(8,128)(2,1)S(1)}, bf16[8,2,128,128]{3,2,1,0:T(8,128)(2,1)S(1)}, u32[]{:S(2)}, u32[]{:S(2)}) collective-permute-start(bf16[8,2,128,128]{3,2,1,0:T(8,128)(2,1)S(1)} %collective-permute-done.9.left.refs_4_.refs_15_), channel_id=1, source_target_pairs={{0,1},{1,0},{4,5},{5,4},{8,9},{9,8},{12,13},{13,12},{2,3},{3,2},{6... | collective-permute-start | bytes 1572872 | tf_op jit(solution)/shard_map/ppermute | solution.py:33
  35.4 2.3 collective-permute-start.12
  35.4 9.5 %collective-permute-start.13 = (bf16[8,2,128,128]{3,2,1,0:T(8,128)(2,1)S(1)}, bf16[8,2,128,128]{3,2,1,0:T(8,128)(2,1)S(1)}, u32[]{:S(2)}, u32[]{:S(2)}) collective-permute-start(bf16[8,2,128,128]{3,2,1,0:T(8,128)(2,1)S(1)} %collective-permute-done.9.left.refs_4_.refs_15_), channel_id=1, source_target_pairs={{0,4},{1,33},{4,8},{5,37},{8,12},{9,41},{12,0},{13,45},{2,6},{3,35... | collective-permute-start | bytes 1572872 | tf_op jit(solution)/shard_map/ppermute | solution.py:33
  44.9 5.1 %collective-permute-start.14 = (bf16[8,2,128,128]{3,2,1,0:T(8,128)(2,1)S(1)}, bf16[8,2,128,128]{3,2,1,0:T(8,128)(2,1)S(1)}, u32[]{:S(2)}, u32[]{:S(2)}) collective-permute-start(bf16[8,2,128,128]{3,2,1,0:T(8,128)(2,1)S(1)} %collective-permute-done.13.refs_6_.refs_17_), channel_id=1, source_target_pairs={{0,1},{1,0},{4,5},{5,4},{8,9},{9,8},{12,13},{13,12},{2,3},{3,2},{6... | collective-permute-start | bytes 1572872 | tf_op jit(solution)/shard_map/ppermute | solution.py:33
